TPU v7x, 32 devices: a whole 2x2x4 slice. The times are simulated.
32 devices in a mesh: dp: 8 (over z, y), tensor: 4 (over x, core).
Axes of the slice: x: 2, y: 2, z: 4, core: 2. Of those that a mesh axis runs over, the one named last changes fastest.
Arguments:
- stream: bfloat16 [32768, 767], P(('dp', 'tensor')), may hold values from -6 to 6
- cotangent: bfloat16 [32768, 767], P(('dp', 'tensor')), may hold values from -6 to 6
- bucket: int32 [8], P('dp'), may hold values from 0 to 2, as said below
- row_counts: int32 [8], P('dp'), may hold values from 1 to 4, as said below
- lengths: int32 [8, 4], P('dp'), may hold values from 0 to 4096, as said below
- w_qkv: bfloat16 [768, 3, 768], P(None, None, 'tensor'), may hold values from -0.3125 to 0.3125
- w_out: bfloat16 [768, 768], P('tensor'), may hold values from -0.75 to 0.75
- w_up: bfloat16 [768, 3072], P(None, 'tensor'), may hold values from -0.21875 to 0.21875
- w_down: bfloat16 [3072, 768], P('tensor'), may hold values from -0.109375 to 0.109375
- gain_one: float32 [768], replicated, may hold values from 0.5 to 1.5
- gain_two: float32 [768], replicated, may hold values from 0.5 to 1.5
Outputs:
- result: bfloat16 [32768, 767], P(('dp', 'tensor'))
- grad_stream: float32 [32768, 767], P(('dp', 'tensor'))
- grad_w_qkv: float32 [768, 3, 768], P(None, None, 'tensor')
- grad_w_out: float32 [768, 768], P('tensor')
- grad_w_up: float32 [768, 3072], P(None, 'tensor')
- grad_w_down: float32 [3072, 768], P('tensor')
- grad_gain_one: float32 [768], replicated
- grad_gain_two: float32 [768], replicated
- root_means: float32 [3], replicated
Inputs may be any that keep to these rules, and one draw needn't show every extreme that they name: Rows of group g have 1024 * 2**bucket[g] slots. row_counts[g] is at most 4096 // (1024 * 2**bucket[g]) and at least half of that. lengths[g, r] lies between half the row's span and the span for r below row_counts[g], and is 0 from there on; the first row of every group is full.
All inputs are finite; a program needn't handle non-finite values.
Results may differ from a plain program's by a relative error of at most 0.013.
The roundings to bfloat16 on the way count: a program that leaves them out, or rounds other values in their place, can miss the bound.
Values may be sent and summed in bfloat16 or wider, within the bound.
No kernel may reach another device: no remote copies, remote signals or barrier semaphores. Data moves between devices by JAX's collectives and lax.ppermute only.
A program may use at most 256 MiB of HBM per device.

v0:
```python
import jax
import jax.numpy as jnp
from jax import lax
from jax.sharding import PartitionSpec as P

HD = 64
BASE = 1024


EPSILON = 1e-05


def decompress(narrow):
    return jnp.concatenate([narrow, -jnp.sum(narrow, axis=1, keepdims=True)], axis=1)


def compress(branch):
    centred = branch - jnp.mean(branch, axis=1, keepdims=True)
    return centred[:, :-1]


def compress_back(gradient):
    padded = jnp.concatenate([gradient, jnp.zeros_like(gradient[:, :1])], axis=1)
    return padded - jnp.mean(padded, axis=1, keepdims=True)


def norm_forward(narrow, gain):
    full = decompress(narrow)
    factor = lax.rsqrt(jnp.mean(full * full, axis=1, keepdims=True) + EPSILON)
    normal_hat = full * factor
    return (normal_hat, factor, (normal_hat * gain).astype(jnp.bfloat16))


def norm_backward(gradient, normal_hat, factor, gain):
    grad_hat = gradient * gain
    grad_full = (
        grad_hat - normal_hat * jnp.mean(grad_hat * normal_hat, axis=1, keepdims=True)
    ) * factor
    return (grad_full[:, :-1] - grad_full[:, -1:], jnp.sum(gradient * normal_hat, axis=0))


def layout(bucket_one, count_one, length_one, slot_total):
    row_span = BASE * jnp.where(bucket_one == 0, 1, jnp.where(bucket_one == 1, 2, 4)).astype(
        jnp.int32
    )
    place = jnp.arange(slot_total, dtype=jnp.int32)
    row_of = place // row_span
    pos_in = place % row_span
    slot_index = jnp.arange(length_one.shape[0], dtype=jnp.int32)
    row_len = jnp.sum(
        jnp.where(row_of[:, None] == slot_index[None, :], length_one[None, :], 0), axis=1
    )
    usable = (row_of < count_one) & (pos_in < row_len)
    return (row_of, pos_in, usable)


def shards(
    stream, cotangent, bucket, row_counts, lengths, w_qkv, w_out, w_up, w_down, gain_one, gain_two
):
    tok_dev = stream.shape[0]
    model_width = stream.shape[1] + 1
    heads_cols = w_qkv.shape[2]
    heads_dev = heads_cols // HD
    tensor_size = lax.axis_size("tensor")
    group_rows = tok_dev * tensor_size
    own_start = lax.axis_index("tensor") * tok_dev
    row_of, pos_in, usable = layout(bucket[0], row_counts[0], lengths[0], group_rows)
    own_mask = lax.dynamic_slice_in_dim(usable, own_start, tok_dev).astype(jnp.float32)[:, None]
    score_scale = HD ** (-0.5)
    stream_f = stream.astype(jnp.float32)
    hat_one, factor_one, normed_one = norm_forward(stream_f, gain_one)
    gathered_one = lax.all_gather(normed_one, "tensor", axis=0, tiled=True)
    flat_qkv = w_qkv.reshape(model_width, 3 * heads_cols)
    packed = jnp.dot(gathered_one, flat_qkv, preferred_element_type=jnp.float32).astype(
        jnp.bfloat16
    )
    packed = packed.reshape(group_rows, 3, heads_dev, HD)
    query_all, key_all, value_all = (packed[:, 0], packed[:, 1], packed[:, 2])
    block_rows = min(512, group_rows)
    block_count = group_rows // block_rows
    index_all = jnp.arange(group_rows, dtype=jnp.int32)

    def blocked(array):
        return array.reshape((block_count, block_rows) + array.shape[1:])

    metadata = (blocked(row_of), blocked(pos_in), blocked(index_all))

    def scores_for(query_blk, row_q, pos_q, index_q):
        scores = (
            jnp.einsum("bhd,khd->hbk", query_blk, key_all, preferred_element_type=jnp.float32)
            * score_scale
        )
        allowed_mask = (
            (row_of[None, :] == row_q[:, None])
            & (pos_in[None, :] <= pos_q[:, None])
            & (usable[None, :] | (index_all[None, :] == index_q[:, None]))
        )
        return jnp.where(allowed_mask[None], scores, -1e30)

    def attend(element):
        query_blk, row_q, pos_q, index_q = element
        scores = scores_for(query_blk, row_q, pos_q, index_q)
        row_max = jnp.max(scores, axis=2, keepdims=True)
        exponent = jnp.exp(scores - row_max)
        row_total = jnp.sum(exponent, axis=2, keepdims=True)
        weights = (exponent / row_total).astype(jnp.bfloat16)
        mixed = jnp.einsum("hbk,khd->bhd", weights, value_all, preferred_element_type=jnp.float32)
        return (mixed.astype(jnp.bfloat16), (row_max + jnp.log(row_total))[:, :, 0])

    attn_blocks, log_totals = lax.map(attend, (blocked(query_all),) + metadata)
    attn_all = attn_blocks.reshape(group_rows, heads_cols)
    branch_attn = lax.psum_scatter(
        jnp.dot(attn_all, w_out, preferred_element_type=jnp.float32),
        "tensor",
        scatter_dimension=0,
        tiled=True,
    )
    middle = stream_f + compress(branch_attn)
    hat_two, factor_two, normed_two = norm_forward(middle, gain_two)
    gathered_two = lax.all_gather(normed_two, "tensor", axis=0, tiled=True)
    pre_act = jnp.dot(gathered_two, w_up, preferred_element_type=jnp.float32)
    hidden = jax.nn.gelu(pre_act).astype(jnp.bfloat16)
    branch_mlp = lax.psum_scatter(
        jnp.dot(hidden, w_down, preferred_element_type=jnp.float32).astype(jnp.bfloat16),
        "tensor",
        scatter_dimension=0,
        tiled=True,
    ).astype(jnp.float32)
    out_f = middle + compress(branch_mlp)
    full_out = decompress(out_f)
    stat_terms = jnp.stack(
        [
            jnp.sum(full_out * full_out * own_mask),
            jnp.sum(branch_attn * branch_attn * own_mask),
            jnp.sum(branch_mlp * branch_mlp * own_mask),
            jnp.sum(own_mask),
        ]
    )
    stat_totals = lax.psum(stat_terms, ("dp", "tensor"))
    grad_out = cotangent.astype(jnp.float32) * own_mask
    grad_mlp = compress_back(grad_out).astype(jnp.bfloat16)
    gathered_grad = lax.all_gather(grad_mlp, "tensor", axis=0, tiled=True)
    grad_down = jnp.einsum("tf,td->fd", hidden, gathered_grad, preferred_element_type=jnp.float32)
    grad_hidden = jnp.einsum("td,fd->tf", gathered_grad, w_down, preferred_element_type=jnp.float32)
    gelu_out, gelu_pull = jax.vjp(jax.nn.gelu, pre_act)
    grad_pre = gelu_pull(grad_hidden)[0].astype(jnp.bfloat16)
    grad_up = jnp.einsum("td,tf->df", gathered_two, grad_pre, preferred_element_type=jnp.float32)
    grad_normed_two = lax.psum_scatter(
        jnp.einsum("tf,df->td", grad_pre, w_up, preferred_element_type=jnp.float32),
        "tensor",
        scatter_dimension=0,
        tiled=True,
    )
    grad_from_two, gain_grad_two = norm_backward(grad_normed_two, hat_two, factor_two, gain_two)
    grad_middle = grad_out + grad_from_two
    grad_attn = compress_back(grad_middle).astype(jnp.bfloat16)
    gathered_attn_grad = lax.all_gather(grad_attn, "tensor", axis=0, tiled=True)
    grad_wout = jnp.einsum(
        "tc,td->cd", attn_all, gathered_attn_grad, preferred_element_type=jnp.float32
    )
    grad_heads = jnp.einsum(
        "td,cd->tc", gathered_attn_grad, w_out, preferred_element_type=jnp.float32
    ).astype(jnp.bfloat16)
    grad_heads = grad_heads.reshape(group_rows, heads_dev, HD)

    def back_step(carry, element):
        key_sum, value_sum = carry
        query_blk, grad_blk, lse_blk, row_q, pos_q, index_q = element
        scores = scores_for(query_blk, row_q, pos_q, index_q)
        probas = jnp.exp(scores - lse_blk[:, :, None])
        value_sum = value_sum + jnp.einsum(
            "hbk,bhd->khd",
            probas.astype(jnp.bfloat16),
            grad_blk,
            preferred_element_type=jnp.float32,
        )
        grad_probs = jnp.einsum(
            "bhd,khd->hbk", grad_blk, value_all, preferred_element_type=jnp.float32
        )
        row_delta = jnp.sum(probas * grad_probs, axis=2, keepdims=True)
        grad_scores = (probas * (grad_probs - row_delta)).astype(jnp.bfloat16)
        grad_query = (
            jnp.einsum("hbk,khd->bhd", grad_scores, key_all, preferred_element_type=jnp.float32)
            * score_scale
        )
        key_sum = (
            key_sum
            + jnp.einsum("hbk,bhd->khd", grad_scores, query_blk, preferred_element_type=jnp.float32)
            * score_scale
        )
        return ((key_sum, value_sum), grad_query)

    zero_heads = jnp.zeros((group_rows, heads_dev, HD), jnp.float32)
    sums_kv, grad_queries = lax.scan(
        back_step,
        (zero_heads, zero_heads),
        (blocked(query_all), blocked(grad_heads), log_totals) + metadata,
    )
    grad_packed = jnp.stack(
        [grad_queries.reshape(group_rows, heads_dev, HD), sums_kv[0], sums_kv[1]], axis=1
    )
    grad_packed = grad_packed.astype(jnp.bfloat16).reshape(group_rows, 3 * heads_cols)
    grad_qkv = jnp.einsum(
        "td,tc->dc", gathered_one, grad_packed, preferred_element_type=jnp.float32
    )
    grad_qkv = grad_qkv.reshape(model_width, 3, heads_cols)
    grad_normed_one = lax.psum_scatter(
        jnp.einsum("tc,dc->td", grad_packed, flat_qkv, preferred_element_type=jnp.float32),
        "tensor",
        scatter_dimension=0,
        tiled=True,
    )
    grad_from_one, gain_grad_one = norm_backward(grad_normed_one, hat_one, factor_one, gain_one)
    grad_input = grad_middle + grad_from_one
    grad_qkv, grad_wout, grad_up, grad_down = lax.psum(
        (grad_qkv, grad_wout, grad_up, grad_down), "dp"
    )
    gain_grad_one, gain_grad_two = lax.psum((gain_grad_one, gain_grad_two), ("dp", "tensor"))
    root_means = jnp.sqrt(stat_totals[:3] / (model_width * stat_totals[3]))
    return (
        out_f.astype(jnp.bfloat16),
        grad_input,
        grad_qkv,
        grad_wout,
        grad_up,
        grad_down,
        gain_grad_one,
        gain_grad_two,
        root_means,
    )


def solution(mesh):
    placed = (
        P(("dp", "tensor"), None),
        P(("dp", "tensor"), None),
        P("dp"),
        P("dp"),
        P("dp", None),
        P(None, None, "tensor"),
        P("tensor", None),
        P(None, "tensor"),
        P("tensor", None),
        P(),
        P(),
    )
    return jax.shard_map(
        shards,
        mesh=mesh,
        in_specs=placed,
        out_specs=(
            P(("dp", "tensor"), None),
            P(("dp", "tensor"), None),
            P(None, None, "tensor"),
            P("tensor", None),
            P(None, "tensor"),
            P("tensor", None),
            P(),
            P(),
            P(),
        ),
        check_vma=False,
    )
```

profile of v0, /device:TPU:0, one launch (start us, length us, event | category | flops | bytes accessed | tf_op | source)
XLA Modules:
  0.0 1964.5 jit_solution(12630586315562302723)
XLA Ops:
  19.8 46.8 %all-gather.5.cloned.1.call-done = bf16[4096,768]{1,0:T(8,128)(2,1)} async-done(((bf16[1024,768]{1,0:T(8,128)(2,1)}), bf16[4096,768]{1,0:T(8,128)(2,1)}) %all-gather.5.cloned.1.call-update) | async-done | bytes 6291472 | tf_op jit(solution)/shard_map/all_gather | solution.py:72
  77.3 323.9 %while.28 = (s32[]{:T(128)}, bf16[8,512,3,64]{1,3,2,0:T(8,128)(2,1)}, f32[8,3,512]{2,1,0:T(4,128)S(1)}, s32[8,512]{1,0:T(8,128)S(1)}, s32[8,512]{1,0:T(8,128)S(1...) while((s32[]{:T(128)}, ...), condition=%wide.region_6.7_spmd.clone, body=%wide.region_3.6_spmd.clone.sunk | while | flops 1698851328 | bytes 93860048 | solution.py:110
  93.3 11.9 fusion.158
  105.2 12.7 fusion.159
  122.0 11.7 fusion.157
  133.7 11.9 fusion.158
  145.6 12.7 fusion.159
  174.0 11.9 fusion.158
  186.0 12.7 fusion.159
  214.4 11.9 fusion.158
  226.4 12.7 fusion.159
  254.8 11.9 fusion.158
  266.8 12.7 fusion.159
  295.2 11.9 fusion.158
  307.1 12.7 fusion.159
  335.6 11.9 fusion.158
  347.5 12.7 fusion.159
  364.3 11.7 fusion.157
  376.0 11.9 fusion.158
  387.9 12.7 fusion.159
  415.3 95.6 %reduce-scatter.5.cloned.1.call-done = f32[1024,768]{1,0:T(8,128)} async-done(((f32[4096,768]{1,0:T(8,128)}), f32[1024,768]{1,0:T(8,128)}) %reduce-scatter.5.cloned.1.call-update) | async-done | bytes 3145744 | tf_op jit(solution)/shard_map/reduce_scatter | solution.py:112
  524.2 35.4 %all-gather.9.cloned.1.call-done = bf16[4096,768]{1,0:T(8,128)(2,1)} async-done(((bf16[1024,768]{1,0:T(8,128)(2,1)}), bf16[4096,768]{1,0:T(8,128)(2,1)}) %all-gather.9.cloned.1.call-update) | async-done | bytes 6291472 | tf_op jit(solution)/shard_map/all_gather | solution.py:142
  570.2 37.7 %all-gather.7.cloned.1.call-done = bf16[4096,768]{1,0:T(8,128)(2,1)} async-done(((bf16[1024,768]{1,0:T(8,128)(2,1)}), bf16[4096,768]{1,0:T(8,128)(2,1)}) %all-gather.7.cloned.1.call-update) | async-done | bytes 6291472 | tf_op jit(solution)/shard_map/all_gather | solution.py:120
  607.9 17.4 fusion.73
  636.1 99.2 %reduce-scatter.9.cloned.1.call-done = f32[1024,768]{1,0:T(8,128)} async-done(((f32[4096,768]{1,0:T(8,128)}), f32[1024,768]{1,0:T(8,128)}) %reduce-scatter.9.cloned.1.call-update) | async-done | bytes 3145744 | tf_op jit(solution)/shard_map/reduce_scatter | solution.py:148
  745.0 12.6 convolution_convert_fusion
  757.6 33.8 %all-gather.11.cloned.1.call-done = bf16[4096,768]{1,0:T(8,128)(2,1)} async-done(((bf16[1024,768]{1,0:T(8,128)(2,1)}), bf16[4096,768]{1,0:T(8,128)(2,1)}) %all-gather.11.cloned.1.call-update) | async-done | bytes 6291472 | tf_op jit(solution)/shard_map/all_gather | solution.py:157
  798.7 794.5 %while.29 = (s32[]{:T(128)}, f32[4096,3,64]{0,2,1:T(8,128)}, f32[4096,3,64]{0,2,1:T(8,128)}, bf16[8,512,3,64]{1,0,3,2:T(8,128)(2,1)}, bf16[8,512,3,64]{1,3,2,0:T...) while((s32[]{:T(128)}, f32[4096,3,64]{0,2,1:T(8,128)}, ...), condition=%wide.region_19.20_spmd.clone, body=%wide.region_17.19_spmd.clone.sunk | while | flops 4137675264 | bytes 228917552 | solution.py:194
  803.6 14.8 fusion.169
  818.4 13.0 fusion.172
  831.4 18.3 multiply_reduce_fusion.10
  849.7 21.9 %multiply_convert_fusion.7 = bf16[3,512,4096]{2,1,0:T(8,128)(2,1)} fusion(f32[3,512,4096]{2,1,0:T(8,128)} %get-tuple-element.655, f32[3,512,4096]{2,1,0:T(8,128)} %fusion.169, f32[3,512]{1,0:T(4,128)S(1)} %get-tuple-element.656, f32[3,512]{1,0:T(4,128)S(1)} %dynamic-slice_bitcast_fusion.2, pred[512,4096]{1,0:T(8,128)(4,1)S(1)} %fusion.170), kind=kLoop, calls=%fused_computation.38.clone.1 | loop fusion | flops 37748736 | bytes 65024000 | tf_op jit(solution)/shard_map/while/body/eval_jaxpr/convert_element_type | solution.py:181
  902.8 13.3 fusion.169
  916.1 13.9 fusion.172
  930.0 18.2 multiply_reduce_fusion.10
  948.2 21.8 %multiply_convert_fusion.7 = bf16[3,512,4096]{2,1,0:T(8,128)(2,1)} fusion(f32[3,512,4096]{2,1,0:T(8,128)} %get-tuple-element.655, f32[3,512,4096]{2,1,0:T(8,128)} %fusion.169, f32[3,512]{1,0:T(4,128)S(1)} %get-tuple-element.656, f32[3,512]{1,0:T(4,128)S(1)} %dynamic-slice_bitcast_fusion.2, pred[512,4096]{1,0:T(8,128)(4,1)S(1)} %fusion.170), kind=kLoop, calls=%fused_computation.38.clone.1 | loop fusion | flops 37748736 | bytes 65024000 | tf_op jit(solution)/shard_map/while/body/eval_jaxpr/convert_element_type | solution.py:181
  1002.1 13.3 fusion.169
  1015.4 13.9 fusion.172
  1029.3 18.2 multiply_reduce_fusion.10
  1047.5 21.8 %multiply_convert_fusion.7 = bf16[3,512,4096]{2,1,0:T(8,128)(2,1)} fusion(f32[3,512,4096]{2,1,0:T(8,128)} %get-tuple-element.655, f32[3,512,4096]{2,1,0:T(8,128)} %fusion.169, f32[3,512]{1,0:T(4,128)S(1)} %get-tuple-element.656, f32[3,512]{1,0:T(4,128)S(1)} %dynamic-slice_bitcast_fusion.2, pred[512,4096]{1,0:T(8,128)(4,1)S(1)} %fusion.170), kind=kLoop, calls=%fused_computation.38.clone.1 | loop fusion | flops 37748736 | bytes 65024000 | tf_op jit(solution)/shard_map/while/body/eval_jaxpr/convert_element_type | solution.py:181
  1101.4 13.3 fusion.169
  1114.7 13.9 fusion.172
  1128.6 18.2 multiply_reduce_fusion.10
  1146.7 21.8 %multiply_convert_fusion.7 = bf16[3,512,4096]{2,1,0:T(8,128)(2,1)} fusion(f32[3,512,4096]{2,1,0:T(8,128)} %get-tuple-element.655, f32[3,512,4096]{2,1,0:T(8,128)} %fusion.169, f32[3,512]{1,0:T(4,128)S(1)} %get-tuple-element.656, f32[3,512]{1,0:T(4,128)S(1)} %dynamic-slice_bitcast_fusion.2, pred[512,4096]{1,0:T(8,128)(4,1)S(1)} %fusion.170), kind=kLoop, calls=%fused_computation.38.clone.1 | loop fusion | flops 37748736 | bytes 65024000 | tf_op jit(solution)/shard_map/while/body/eval_jaxpr/convert_element_type | solution.py:181
  1200.6 13.3 fusion.169
  1213.9 13.9 fusion.172
  1227.8 18.2 multiply_reduce_fusion.10
  1246.0 21.8 %multiply_convert_fusion.7 = bf16[3,512,4096]{2,1,0:T(8,128)(2,1)} fusion(f32[3,512,4096]{2,1,0:T(8,128)} %get-tuple-element.655, f32[3,512,4096]{2,1,0:T(8,128)} %fusion.169, f32[3,512]{1,0:T(4,128)S(1)} %get-tuple-element.656, f32[3,512]{1,0:T(4,128)S(1)} %dynamic-slice_bitcast_fusion.2, pred[512,4096]{1,0:T(8,128)(4,1)S(1)} %fusion.170), kind=kLoop, calls=%fused_computation.38.clone.1 | loop fusion | flops 37748736 | bytes 65024000 | tf_op jit(solution)/shard_map/while/body/eval_jaxpr/convert_element_type | solution.py:181
  1299.9 13.3 fusion.169
  1313.1 13.9 fusion.172
  1327.0 18.2 multiply_reduce_fusion.10
  1345.2 21.8 %multiply_convert_fusion.7 = bf16[3,512,4096]{2,1,0:T(8,128)(2,1)} fusion(f32[3,512,4096]{2,1,0:T(8,128)} %get-tuple-element.655, f32[3,512,4096]{2,1,0:T(8,128)} %fusion.169, f32[3,512]{1,0:T(4,128)S(1)} %get-tuple-element.656, f32[3,512]{1,0:T(4,128)S(1)} %dynamic-slice_bitcast_fusion.2, pred[512,4096]{1,0:T(8,128)(4,1)S(1)} %fusion.170), kind=kLoop, calls=%fused_computation.38.clone.1 | loop fusion | flops 37748736 | bytes 65024000 | tf_op jit(solution)/shard_map/while/body/eval_jaxpr/convert_element_type | solution.py:181
  1399.1 13.3 fusion.169
  1412.4 13.9 fusion.172
  1426.3 18.2 multiply_reduce_fusion.10
  1444.4 21.8 %multiply_convert_fusion.7 = bf16[3,512,4096]{2,1,0:T(8,128)(2,1)} fusion(f32[3,512,4096]{2,1,0:T(8,128)} %get-tuple-element.655, f32[3,512,4096]{2,1,0:T(8,128)} %fusion.169, f32[3,512]{1,0:T(4,128)S(1)} %get-tuple-element.656, f32[3,512]{1,0:T(4,128)S(1)} %dynamic-slice_bitcast_fusion.2, pred[512,4096]{1,0:T(8,128)(4,1)S(1)} %fusion.170), kind=kLoop, calls=%fused_computation.38.clone.1 | loop fusion | flops 37748736 | bytes 65024000 | tf_op jit(solution)/shard_map/while/body/eval_jaxpr/convert_element_type | solution.py:181
  1498.3 13.3 fusion.169
  1511.6 13.9 fusion.172
  1525.5 18.2 multiply_reduce_fusion.10
  1543.7 21.8 %multiply_convert_fusion.7 = bf16[3,512,4096]{2,1,0:T(8,128)(2,1)} fusion(f32[3,512,4096]{2,1,0:T(8,128)} %get-tuple-element.655, f32[3,512,4096]{2,1,0:T(8,128)} %fusion.169, f32[3,512]{1,0:T(4,128)S(1)} %get-tuple-element.656, f32[3,512]{1,0:T(4,128)S(1)} %dynamic-slice_bitcast_fusion.2, pred[512,4096]{1,0:T(8,128)(4,1)S(1)} %fusion.170), kind=kLoop, calls=%fused_computation.38.clone.1 | loop fusion | flops 37748736 | bytes 65024000 | tf_op jit(solution)/shard_map/while/body/eval_jaxpr/convert_element_type | solution.py:181
  1619.7 14.7 fusion.95
  1656.4 52.4 %reduce-scatter.11.cloned.1.call-done = f32[1024,768]{1,0:T(8,128)} async-done(((f32[4096,768]{1,0:T(8,128)}), f32[1024,768]{1,0:T(8,128)}) %reduce-scatter.11.cloned.1.call-update) | async-done | bytes 3145744 | tf_op jit(solution)/shard_map/reduce_scatter | solution.py:207
  1712.6 42.0 %all-reduce.2 = (f32[768]{0:T(1024)}, f32[768]{0:T(1024)}, f32[4]{0:T(128)S(1)}) all-reduce(f32[768]{0:T(1024)S(1)} %get-tuple-element.347, f32[768]{0:T(1024)S(1)} %copy-done.33, f32[4]{0:T(128)S(1)} %pad_maximum_fusion.2), channel_id=1, replica_groups=mesh['dp'=8,'tensor'=4] {'dp','tensor'}, use_global_device_ids=true, to_apply=%region_27.28 | all-reduce | flops 1540 | bytes 12320 | tf_op jit(solution)/shard_map/psum | solution.py:218
  1762.7 188.5 %all-reduce.6.cloned.1.call-done = (f32[768,3,192]{0,2,1:T(8,128)}, f32[192,768]{1,0:T(8,128)}, f32[768,768]{1,0:T(8,128)}, f32[768,768]{1,0:T(8,128)}) async-done(((f32[768,3,192]{0,2,1:T(8,128)}, f32[192,768]{1,0:T(8,128)}, f32[768,768]{1,0:T(8,128)}, f32[768,768]{1,0:T(8,128)}), (f32[768,3,192]{0,2,1:T(8,128)}, f32[192,768]{1,0:T(8,128)}, f32[768,768]{1,0:T(8,128)}, ...) | async-done | bytes 7077904 | tf_op jit(solution)/shard_map/psum | solution.py:215
  (349 shorter events, 511.7 us)
Async XLA Ops:
  7.2 600.8 %copy-start = (bf16[768,768]{1,0:T(8,128)(2,1)S(1)}, bf16[768,768]{1,0:T(8,128)(2,1)}, u32[]{:S(2)}) copy-start(bf16[768,768]{1,0:T(8,128)(2,1)} %param.22) | copy-start | bytes 3538948
  7.2 59.4 %all-gather.5.cloned.1.call-start = ((), (), s32[]{:S(2)}) async-start(), calls=%async_computation.4 | async-start | bytes 7864320 | tf_op jit(solution)/shard_map/all_gather | solution.py:72
  12.3 3.4 copy-start.31
  12.6 4.8 copy-start.13
  12.6 3.2 copy-start.7
  15.7 3.6 copy-start.34
  15.7 50.9 %copy-start.36 = (bf16[768,3,192]{0,2,1:T(8,128)(2,1)S(1)}, bf16[768,3,192]{0,2,1:T(8,128)(2,1)}, u32[]{:S(2)}) copy-start(bf16[768,3,192]{0,2,1:T(8,128)(2,1)} %param.20) | copy-start | bytes 2654212
  17.4 493.6 %reduce-scatter.5.cloned.1.call-start = ((), (), s32[]{:S(2)}) async-start(), calls=%async_computation.5 | async-start | bytes 15728640 | tf_op jit(solution)/shard_map/reduce_scatter | solution.py:112
  93.3 11.9 copy-start.8
  133.7 11.9 copy-start.8
  174.0 11.9 copy-start.8
  214.4 11.9 copy-start.8
  254.8 11.9 copy-start.8
  295.2 11.9 copy-start.8
  335.6 11.9 copy-start.8
  376.0 11.9 copy-start.8
  401.1 4.2 copy-start.24
  411.8 147.8 %all-gather.9.cloned.1.call-start = ((), (), s32[]{:S(2)}) async-start(), calls=%async_computation.8 | async-start | bytes 7864320 | tf_op jit(solution)/shard_map/all_gather | solution.py:142
  411.8 329.2 %copy-start.26 = (f32[1024]{0:T(1024)}, f32[1024]{0:T(1024)S(1)}, u32[]{:S(2)}) copy-start(f32[1024]{0:T(1024)S(1)} %dynamic-slice_convert_fusion) | copy-start | bytes 12292
  415.3 192.7 %all-gather.7.cloned.1.call-start = ((), (), s32[]{:S(2)}) async-start(), calls=%async_computation.6 | async-start | bytes 7864320 | tf_op jit(solution)/shard_map/all_gather | solution.py:120
  510.9 3.6 copy-start.12
  518.6 3.1 copy-start.30
  518.9 3.6 copy-start.4
  524.1 211.1 %reduce-scatter.9.cloned.1.call-start = ((), (), s32[]{:S(2)}) async-start(), calls=%async_computation.9 | async-start | bytes 15728640 | tf_op jit(solution)/shard_map/reduce_scatter | solution.py:148
  625.3 2.6 copy-start.38
  636.0 155.4 %all-gather.11.cloned.1.call-start = ((), (), s32[]{:S(2)}) async-start(), calls=%async_computation.10 | async-start | bytes 7864320 | tf_op jit(solution)/shard_map/all_gather | solution.py:157
  735.2 4.5 copy-start.5
  735.2 4.7 copy-start.15
  741.8 1.6 copy-start.9
  743.5 1.5 copy-start.35
  744.9 897.6 %reduce-scatter.7.cloned.1.call-start = ((), (), s32[]{:S(2)}) async-start(), calls=%async_computation.7 | async-start | bytes 7864320 | tf_op jit(solution)/shard_map/reduce_scatter | solution.py:123
  757.5 33.9 %copy-start.25 = (bf16[192,768]{1,0:T(8,128)(2,1)S(1)}, bf16[192,768]{1,0:T(8,128)(2,1)}, u32[]{:S(2)}) copy-start(bf16[192,768]{1,0:T(8,128)(2,1)} %param.21) | copy-start | bytes 884740
  757.6 951.2 %reduce-scatter.11.cloned.1.call-start = ((), (), s32[]{:S(2)}) async-start(), calls=%async_computation.11 | async-start | bytes 15728640 | tf_op jit(solution)/shard_map/reduce_scatter | solution.py:207
  880.5 17.6 copy-start.3
  978.9 18.5 copy-start.3
  1078.2 18.5 copy-start.3
  1177.4 18.5 copy-start.3
  1276.6 18.5 copy-start.3
  1375.9 18.5 copy-start.3
  1475.1 18.5 copy-start.3
  1574.3 18.5 copy-start.3
  1595.8 5.5 copy-start.37
  1599.2 2.1 copy-start.20
  1609.4 341.8 %all-reduce.6.cloned.1.call-start = ((), (), s32[]{:S(2)}) async-start(), calls=%async_computation.12 | async-start | bytes 14155776 | tf_op jit(solution)/shard_map/psum | solution.py:215
  1609.5 24.9 %slice-start.4 = ((s8[6291456]{0:T(1024)(128)(4,1)}), s8[4194304]{0:T(1024)(128)(4,1)S(1)}, s32[]{:S(2)}) async-start(s8[6291456]{0:T(1024)(128)(4,1)} %bitcast.195), calls=%async_computation.17 | async-start | bytes 8388608
  1609.5 27.2 %slice-start = ((s8[4718592]{0:T(1024)(128)(4,1)}), s8[4194304]{0:T(1024)(128)(4,1)S(1)}, s32[]{:S(2)}) async-start(s8[4718592]{0:T(1024)(128)(4,1)} %bitcast.178), calls=%async_computation.13 | async-start | bytes 8388608
  1609.5 27.2 %slice-start.2 = ((s8[6291456]{0:T(1024)(128)(4,1)}), s8[4194304]{0:T(1024)(128)(4,1)S(1)}, s32[]{:S(2)}) async-start(s8[6291456]{0:T(1024)(128)(4,1)} %bitcast.193), calls=%async_computation.15 | async-start | bytes 8388608
  1619.7 14.7 copy-start.17
  1619.7 14.7 slice-start.5
  1619.7 17.0 slice-start.1
  1619.7 17.0 slice-start.3
  1641.9 2.4 copy-start.27
  1642.5 1.9 copy-start.18
  1642.5 3.5 copy-start.6
  1648.4 3.7 copy-start.11
  1648.5 60.3 %copy-start.14 = (f32[1024,1]{1,0:T(8,128)S(1)}, f32[1024,1]{1,0:T(8,128)}, u32[]{:S(2)}) copy-start(f32[1024,1]{1,0:T(8,128)} %copy-done.13) | copy-start | bytes 12292
  1648.5 60.3 %copy-start.29 = (f32[1024]{0:T(1024)S(1)}, f32[1024]{0:T(1024)}, u32[]{:S(2)}) copy-start(f32[1024]{0:T(1024)} %copy-done.28) | copy-start | bytes 12292
  1648.5 60.3 %copy-start.32 = (f32[768]{0:T(1024)S(1)}, f32[768]{0:T(1024)}, u32[]{:S(2)}) copy-start(f32[768]{0:T(1024)} %param.24) | copy-start | bytes 9220
  1656.4 56.2 %copy-start.33 = (f32[768]{0:T(1024)S(1)}, f32[768]{0:T(1024)}, u32[]{:S(2)}) copy-start(f32[768]{0:T(1024)} %get-tuple-element.345) | copy-start | bytes 9220
  1755.8 4.8 copy-start.10
  1951.2 3.0 copy-start.23
  1951.2 3.8 copy-start.22
  1954.2 2.2 copy-start.21
  1955.0 2.8 copy-start.1
  (11 other events, 12.4 us)
Sparse Core Ops, SparseCore 0:
  17.5 49.0 all-gather.4
  411.9 99.0 reduce-scatter.4
  513.1 46.3 all-gather.8
  561.5 46.3 all-gather.6
  636.1 99.0 reduce-scatter.8
  745.0 46.3 all-gather.10
  794.0 58.3 reduce-scatter.6
  1609.5 99.2 reduce-scatter.10
  1714.4 236.7 all-reduce.5
where the time goes:
time: 1970 us; the launch traced here: 1960 us
  matrix products  814 us (41%)
  waiting for transfers between devices  590 us (30%)
  other arithmetic  394 us (20%)
  local copies, waits for them, and re-layouts  106 us (5%)
  blocking collectives  42 us (2%)
    dot_general x16, matrix products, scores_for(): jnp.einsum('bhd,khd->hbk', query_blk, key_all, preferred_element_type=jnp...  201 us
    psum x1, waiting for transfers between devices, shards(): lax.psum((grad_qkv, grad_wout, grad_up, grad_down), 'dp')  189 us
    convert_element_type x8, other arithmetic, back_step(): grad_scores = (probas * (grad_probs - row_delta)).astype(jnp.bfloat16)  174 us
    dot_general x8, matrix products, back_step(): jnp.einsum('bhd,khd->hbk', grad_blk, value_all, preferred_element_type=jn...  145 us
    dot_general x8, matrix products, back_step(): jnp.einsum('hbk,bhd->khd', probas.astype(jnp.bfloat16), grad_blk, preferr...  110 us
    dot_general x8, matrix products, attend(): jnp.einsum('hbk,khd->bhd', weights, value_all, preferred_element_type=jnp...  101 us
    reduce_scatter x1, waiting for transfers between devices, shards(): lax.psum_scatter(jnp.einsum('tf,df->td', grad_pre, w_up, preferred_elemen...  99.2 us
    reduce_scatter x1, waiting for transfers between devices, shards(): lax.psum_scatter(jnp.dot(attn_all, w_out, preferred_element_type=jnp.floa...  95.6 us
  transfers between devices with their start and end apart: 9, of which 8 were waited for; matrix products, arithmetic and copies ran while one was open for 46% of the time, Pallas kernels for 0%

commit v1 on v0

v1 whole, which is shorter than its diff:
```python
import functools
import jax, jax.numpy as jnp, numpy as np
from jax import lax
from jax.experimental import pallas as pl
from jax.experimental.pallas import tpu as pltpu
from jax.sharding import PartitionSpec as P
HD=64; BASE=1024
LANES=128
SHIFT_LIMIT=70.0
F32=jnp.float32; BF=jnp.bfloat16
NT=(((1,),(1,)),((),()))
NN=(((1,),(0,)),((),()))
def dot(a,b,dims): return lax.dot_general(a,b,dims,preferred_element_type=F32)

def tables(nh, wide):
    cols=nh*HD; lane=np.arange(wide)
    head=np.where(lane<cols,lane//HD,np.where(lane<cols+4*nh,(lane-cols)//4,-1))
    spare=(lane>=cols)&(lane<cols+4*nh)
    masks=np.zeros((8,wide),np.float32)
    for h in range(nh): masks[h]=(head==h)
    masks[nh]=spare
    for h in range(nh): masks[nh+1+h]=spare&(head==h)
    fold=np.zeros((wide,LANES),np.float32)
    hi=wide-LANES
    same=(head[:,None]==head[None,hi:])&(head[:,None]>=0)
    fold[:]=same&(lane<cols)[:,None]&spare[None,hi:]
    spread=np.zeros((LANES,wide),np.float32)
    spread[:]=(same&(lane<cols)[:,None]&spare[None,hi:]).T
    return jnp.asarray(masks,BF),jnp.asarray(fold,BF),jnp.asarray(spread,BF)

def row_info(sc_ref, start):
    span=sc_ref[1]
    row=start//span
    length=sc_ref[3]
    for r in range(1,4):
        length=jnp.where(row==r, sc_ref[3+r], length)
    length=jnp.where(row<sc_ref[2], length, 0)
    return row*span, row*span+length, row*span+span

def place(sc_ref, start, shard):
    return pl.multiple_of((jnp.bitwise_xor(start//shard, sc_ref[0]))*shard + start%shard, 256)

def parts(x, cols, hi):
    lane=lax.broadcasted_iota(jnp.int32,x.shape,1)+hi-cols
    which=jnp.where(lane<0,3,lane%4)
    a=x.astype(BF).astype(F32); r=x-a; b=r.astype(BF).astype(F32); c=r-b
    return jnp.where(which==0,a,jnp.where(which==1,b,jnp.where(which==2,c,0.0))).astype(BF)

def fwd_kernel(nh, bq, shard, sc_ref, p_ref, mask_ref, fold_ref, spread_ref, o_ref, qx_ref, q_s, k_s, v_s, kn_s, sh_s, a_s):
    T=p_ref.shape[0]; W=p_ref.shape[1]//3; hi=W-LANES; cols=nh*HD
    i=pl.program_id(0)
    @pl.when(i==0)
    def _():
        kn=jnp.zeros((8,LANES),F32)
        for c in range(0,T,512):
            k=p_ref[c:c+512,W:2*W]; v=p_ref[c:c+512,2*W:]
            k_s[c:c+512,:]=k+mask_ref[nh:nh+1,:]
            kn=jnp.maximum(kn,jnp.max(dot(k*k,fold_ref[...],NN).reshape(64,8,LANES),axis=0))
            for h in range(nh):
                v_s[h,c:c+512,:]=v*mask_ref[h:h+1,:]+mask_ref[nh+1+h:nh+2+h,:]
        kn_s[...]=jnp.broadcast_to(jnp.max(kn,axis=0,keepdims=True),(8,LANES))
    start=i*bq
    row_start,valid_end,_=row_info(sc_ref,start)
    at=place(sc_ref,start,shard)
    q=p_ref[pl.ds(at,bq),:W]; own=p_ref[pl.ds(at,bq),W:2*W]
    before=(start-row_start)//bq
    full=jnp.minimum(before,(valid_end-row_start)//bq)
    some=jnp.minimum(before,(valid_end-row_start+bq-1)//bq)
    rows=lax.broadcasted_iota(jnp.int32,(bq,bq),0); tcol=lax.broadcasted_iota(jnp.int32,(bq,bq),1)
    diag=(tcol==rows)|((tcol<rows)&(tcol<valid_end-start))
    def set_q(shift_lanes):
        x=jnp.concatenate([q[:,:hi],q[:,hi:]+shift_lanes],axis=1)
        for h in range(nh): q_s[h]=x*mask_ref[h:h+1,:]
    self_score=dot(q*own,fold_ref[...],NN)
    shift=self_score.astype(BF).astype(F32)
    sh_s[...]=shift
    set_q(parts(-shift,cols,hi))
    size=jnp.sqrt(dot(q*q,fold_ref[...],NN)*kn_s[:1,:])*1.02
    bounded=jnp.max(size-shift)<=SHIFT_LIMIT
    @pl.when(jnp.logical_not(bounded))
    def _():
        lane=lax.broadcasted_iota(jnp.int32,(bq,LANES),1)+hi-cols
        new=jnp.zeros((bq,LANES),F32)
        for h in range(nh):
            qh=q*mask_ref[h:h+1,:]
            m0=jnp.max(jnp.where(diag,dot(qh,k_s[pl.ds(at,bq),:],NT),-1e30),axis=1,keepdims=True)
            def look(j,m):
                b=row_start+j*bq
                s=dot(qh,k_s[pl.ds(place(sc_ref,b,shard),bq),:],NT)
                s=jnp.where(tcol<valid_end-b,s,-1e30)
                return jnp.maximum(m,jnp.max(s,axis=1,keepdims=True))
            m=lax.fori_loop(0,some,look,m0)
            new=jnp.where((lane>=4*h)&(lane<4*h+4),m,new)
        sh_s[...]=new
        set_q(parts(-new,cols,hi))
    def step(b,masking,first):
        bt=place(sc_ref,b,shard)
        k=k_s[pl.ds(bt,bq),:]
        ps=[]
        for h in range(nh):
            s=dot(q_s[h],k,NT)
            if masking is not None: s=jnp.where(masking,s,-1e30)
            ps.append(jnp.exp(s).astype(BF))
        new=dot(jnp.concatenate(ps,axis=1),v_s[:,pl.ds(bt,bq),:].reshape(nh*bq,W),NN)
        if first: a_s[...]=new
        else: a_s[...]+=new
    step(start,diag,True)
    def whole(j,c):
        step(row_start+j*bq,None,False); return c
    def partly(j,c):
        b=row_start+j*bq
        step(b,tcol<valid_end-b,False); return c
    lax.fori_loop(0,full,whole,0)
    lax.fori_loop(full,some,partly,0)
    total=a_s[:,hi:]
    lane=lax.broadcasted_iota(jnp.int32,(bq,LANES),1)+hi-cols
    spare=(lane>=0)&(lane<4*nh)
    total=jnp.where(spare,total,1.0)
    o_ref[...]=(a_s[:,:cols]*dot(parts(1.0/total,cols,hi),spread_ref[...],NN)[:,:cols]).astype(BF)
    lse=jnp.where(spare,sh_s[...]+jnp.log(total),0.0)
    qx_ref[...]=jnp.concatenate([q[:,:hi],q[:,hi:]+parts(-lse,cols,hi)],axis=1)

def const(a): return pl.BlockSpec(a.shape,lambda i,sc:(0,)*a.ndim)

def attn_fwd(scal, packed, shard, nh=3, bq=512):
    T=packed.shape[0]; W=packed.shape[1]//3
    tabs=tables(nh,W)
    def where(i,sc):
        per=shard//bq
        return (jnp.bitwise_xor(i//per,sc[0])*per+i%per,0)
    return pl.pallas_call(
        functools.partial(fwd_kernel,nh,bq,shard),
        grid_spec=pltpu.PrefetchScalarGridSpec(num_scalar_prefetch=1,grid=(T//bq,),
            in_specs=[const(packed)]+[const(a) for a in tabs],
            out_specs=[pl.BlockSpec((bq,nh*HD),where),pl.BlockSpec((bq,W),where)],
            scratch_shapes=[pltpu.VMEM((nh,bq,W),BF),pltpu.VMEM((T,W),BF),pltpu.VMEM((nh,T,W),BF),
                pltpu.VMEM((8,LANES),F32),pltpu.VMEM((bq,LANES),F32),pltpu.VMEM((bq,W),F32)]),
        out_shape=[jax.ShapeDtypeStruct((T,nh*HD),BF),jax.ShapeDtypeStruct((T,W),BF)],
        compiler_params=pltpu.CompilerParams(vmem_limit_bytes=56*2**20),
        name="attention_forward",
    )(scal,packed,*tabs)

def bwd_kernel(nh,bk,shard,sc_ref,qx_ref,p_ref,o_ref,g_ref,mask_ref,fold_ref,out_ref,q_s,d_s,dq_s,dk_s,dv_s):
    T=p_ref.shape[0]; W=p_ref.shape[1]//3; hi=W-LANES; cols=nh*HD
    j=pl.program_id(0)
    @pl.when(j==0)
    def _():
        for c in range(0,T,512):
            qx=qx_ref[c:c+512,:]
            g=g_ref[c:c+512,:]
            og=o_ref[c:c+512,:].astype(F32)*g.astype(F32)
            og1=og.astype(BF); og2=(og-og1.astype(F32)).astype(BF)
            delta=dot(og1,fold_ref[:cols,:],NN)+dot(og2,fold_ref[:cols,:],NN)
            gx=jnp.concatenate([g,jnp.zeros((512,W-cols),BF)],axis=1)
            gx=jnp.concatenate([gx[:,:hi],gx[:,hi:]+parts(-delta,cols,hi)],axis=1)
            for h in range(nh):
                q_s[h,c:c+512,:]=qx*mask_ref[h:h+1,:]
                d_s[h,c:c+512,:]=gx*mask_ref[h:h+1,:]
            dq_s[:,c:c+512]=jnp.zeros((cols,512),F32)
    start=j*bk
    row_start,valid_end,row_end=row_info(sc_ref,start)
    at=place(sc_ref,start,shard)
    k0=p_ref[pl.ds(at,bk),W:2*W]
    k=k0+mask_ref[nh:nh+1,:]; v=p_ref[pl.ds(at,bk),2*W:]+mask_ref[nh:nh+1,:]
    kt=jnp.transpose(k0)
    def step(i,kind):
        b=start+i*bk
        bt=place(sc_ref,b,shard)
        if kind!=0:
            krow=lax.broadcasted_iota(jnp.int32,(bk,bk),0); qcol=lax.broadcasted_iota(jnp.int32,(bk,bk),1)
            ok=krow<valid_end-start
            if kind==2: ok=(krow==qcol)|((krow<qcol)&ok)
        ps=[];dss=[]
        for h in range(nh):
            s=dot(k,q_s[h,pl.ds(bt,bk),:],NT)
            if kind!=0: s=jnp.where(ok,s,-1e30)
            p=jnp.exp(s)
            ds=(p*dot(v,d_s[h,pl.ds(bt,bk),:],NT)).astype(BF)
            ps.append(p.astype(BF)); dss.append(ds)
            dq_s[h*HD:(h+1)*HD,pl.ds(bt,bk)]+=dot(kt[h*HD:(h+1)*HD],ds,NN)
        dv=dot(jnp.concatenate(ps,axis=1),d_s[:,pl.ds(bt,bk),:].reshape(nh*bk,W),NN)
        dk=dot(jnp.concatenate(dss,axis=1),q_s[:,pl.ds(bt,bk),:].reshape(nh*bk,W),NN)
        if kind==2: dv_s[...]=dv; dk_s[...]=dk
        else: dv_s[...]+=dv; dk_s[...]+=dk
    after=(row_end-start)//bk
    n_off=jnp.where(valid_end>start,after,1)
    step(0,2)
    whole=valid_end>=start+bk
    lax.fori_loop(1,jnp.where(whole,after,1),lambda i,c:(step(i,0),c)[1],0)
    lax.fori_loop(1,jnp.where(whole,1,n_off),lambda i,c:(step(i,1),c)[1],0)
    keep=(lax.broadcasted_iota(jnp.int32,(bk,W),1)<cols)
    out_ref[pl.ds(at,bk),W:2*W]=jnp.where(keep,dk_s[...],0.0).astype(BF)
    out_ref[pl.ds(at,bk),2*W:]=jnp.where(keep,dv_s[...],0.0).astype(BF)
    @pl.when(j==pl.num_programs(0)-1)
    def _():
        for c in range(0,T,512):
            x=jnp.concatenate([dq_s[:,c:c+512],jnp.zeros((W-cols,512),F32)],axis=0)
            out_ref[c:c+512,:W]=jnp.transpose(x).astype(BF)

def attn_bwd(scal,qx,packed,attn,grad,shard,nh=3,bk=512):
    T=packed.shape[0]; W=packed.shape[1]//3
    masks,fold,spread=tables(nh,W)
    return pl.pallas_call(
        functools.partial(bwd_kernel,nh,bk,shard),
        grid_spec=pltpu.PrefetchScalarGridSpec(num_scalar_prefetch=1,grid=(T//bk,),
            in_specs=[const(qx),const(packed),const(attn),const(grad),const(masks),const(fold)],
            out_specs=const(packed),
            scratch_shapes=[pltpu.VMEM((nh,T,W),BF),pltpu.VMEM((nh,T,W),BF),pltpu.VMEM((nh*HD,T),F32),
                pltpu.VMEM((bk,W),F32),pltpu.VMEM((bk,W),F32)]),
        out_shape=jax.ShapeDtypeStruct(packed.shape,BF),
        compiler_params=pltpu.CompilerParams(vmem_limit_bytes=60*2**20),
        name="attention_backward",
    )(scal,qx,packed,attn,grad,masks,fold)


EPSILON = 1e-05
TN=(((0,),(0,)),((),()))
VMEM_LIMIT=60*2**20


def widen(ref, buf):
    buf[:,:ref.shape[1]]=ref[...].astype(F32)
    lane=lax.broadcasted_iota(jnp.int32,buf.shape,1)
    return jnp.where(lane<ref.shape[1],buf[...],0.0)

def closed(x):
    lane=lax.broadcasted_iota(jnp.int32,x.shape,1)
    return jnp.where(lane<x.shape[1]-1,x,-jnp.sum(x,axis=1,keepdims=True))

def last_off(x):
    return x-x[:,x.shape[1]-1:]

def centred(x):
    return x-jnp.mean(x,axis=1,keepdims=True)

def inverse(z):
    return lax.rsqrt(jnp.mean(z*z,axis=1,keepdims=True)+EPSILON)

def norm_pull(grad,hat,inv,gain):
    dh=grad*gain
    return last_off((dh-hat*jnp.mean(dh*hat,axis=1,keepdims=True))*inv)

def first_norm_kernel(x_ref,gain_ref,n_ref,buf):
    z=closed(widen(x_ref,buf))
    n_ref[...]=(z*inverse(z)*gain_ref[...]).astype(BF)

def first_norm(stream,gain):
    T,C=stream.shape; R=min(T,256)
    return pl.pallas_call(first_norm_kernel,grid=(T//R,),
        in_specs=[pl.BlockSpec((R,C),lambda i:(i,0)),pl.BlockSpec((1,C+1),lambda i:(0,0))],
        out_specs=pl.BlockSpec((R,C+1),lambda i:(i,0)),
        out_shape=jax.ShapeDtypeStruct((T,C+1),BF),
        scratch_shapes=[pltpu.VMEM((R,C+1),F32)],name="first_norm")(stream,gain)

def last_norm_kernel(x_ref,mid_ref,own_ref,far_ref,gain_ref,out_ref,buf):
    z=closed(widen(x_ref,buf))
    inv=inverse(z)
    grad=own_ref[...].astype(F32)+far_ref[...].astype(F32)
    out=mid_ref[...]+norm_pull(grad,z*inv,inv,gain_ref[...])
    out_ref[...]=out[:,:out_ref.shape[1]]

def last_norm(stream,middle,own,far,gain):
    T,C=stream.shape; R=min(T,256)
    row=lambda w: pl.BlockSpec((R,w),lambda i:(i,0))
    return pl.pallas_call(last_norm_kernel,grid=(T//R,),
        in_specs=[row(C),row(C+1),row(C+1),row(C+1),pl.BlockSpec((1,C+1),lambda i:(0,0))],
        out_specs=row(C),out_shape=jax.ShapeDtypeStruct((T,C),F32),
        scratch_shapes=[pltpu.VMEM((R,C+1),F32)],name="last_norm")(stream,middle,own,far,gain)

def middle_kernel(n,tiles,sc_ref,x_ref,c_ref,gain_ref,*refs):
    attn=refs[:n]; weights=refs[n:2*n]
    res_ref,mid_ref,gh_ref,gw_ref,go_ref,sum_ref,buf,z_s,n_s,g_s,bm_s,gn_s=refs[2*n:]
    T,D=z_s.shape; H=attn[0].shape[1]; FD=(weights[0].shape[0]-H)//2; R=T//tiles
    k=pl.program_id(0)
    def valid_rows(r):
        span=sc_ref[1]
        at=sc_ref[16]+r*R+lax.broadcasted_iota(jnp.int32,(R,1),0)
        row=at//span
        length=jnp.zeros((R,1),jnp.int32)
        for s in range(4): length=jnp.where(row==s,sc_ref[3+s],length)
        return (row<sc_ref[2])&(at-row*span<length)
    def grad_out(r):
        buf[:,:D-1]=c_ref[r*R:(r+1)*R,:].astype(F32)
        lane=lax.broadcasted_iota(jnp.int32,(R,D),1)
        return jnp.where((lane<D-1)&valid_rows(r),buf[...],0.0)
    def squares(x,r):
        x=jnp.where(valid_rows(r),x,0.0)
        return jnp.sum((x*x).reshape(R//8,8,D),axis=0)
    @pl.when(k==0)
    def _():
        for r in range(tiles):
            at=slice(r*R,(r+1)*R)
            buf[:,:D-1]=x_ref[at,:].astype(F32)
            lane=lax.broadcasted_iota(jnp.int32,(R,D),1)
            z1=closed(jnp.where(lane<D-1,buf[...],0.0))
            ba=sum(dot(attn[s][at,:],weights[s][:H,:],NN) for s in range(n))
            z2=z1+centred(ba)
            z_s[at,:]=z2
            n_s[at,:]=(z2*inverse(z2)*gain_ref[...]).astype(BF)
            g_s[at,:]=centred(grad_out(r)).astype(BF)
            sq=squares(ba,r)
            if r==0: sum_ref[16:24,:]=sq
            else: sum_ref[16:24,:]+=sq
    def piece(s):
        w=weights[s]
        up=w[H:H+FD,:]; down=w[H+FD:,:]
        for r in range(tiles):
            at=slice(r*R,(r+1)*R)
            nr=n_s[at,:]; gr=g_s[at,:]
            x=dot(nr,up,NN)
            th=jnp.tanh(0.7978845608028654*(x+0.044715*x*x*x))
            half=0.5*(1.0+th)
            hid=(x*half).astype(BF)
            slope=half+0.5*x*(1.0-th*th)*(0.7978845608028654*(1.0+0.134145*x*x))
            gp=(dot(gr,down,NT)*slope).astype(BF)
            bm=dot(hid,down,NN); gn=dot(gp,up,NT)
            if s==0: bm_s[at,:]=bm; gn_s[at,:]=gn
            else: bm_s[at,:]+=bm; gn_s[at,:]+=gn
            gu=dot(nr,gp,TN); gd=dot(hid,gr,TN)
            if r==0: wu,wd=gu,gd
            else: wu,wd=wu+gu,wd+gd
        gw_ref[0,:FD,:]=wu.astype(BF); gw_ref[0,FD:,:]=wd.astype(BF)
    for s in range(n): pl.when(k==s)(functools.partial(piece,s))
    @pl.when(k==n-1)
    def _():
        for r in range(tiles):
            at=slice(r*R,(r+1)*R)
            z2=z_s[at,:]; inv=inverse(z2); hat=z2*inv; gn=gn_s[at,:]; bm=bm_s[at,:]
            out=z2+centred(bm)
            res_ref[at,:]=out[:,:D-1].astype(BF)
            mid=grad_out(r)+norm_pull(gn,hat,inv,gain_ref[...])
            mid_ref[at,:]=mid
            ga=centred(mid).astype(BF)
            g_s[at,:]=ga
            for s in range(n): gh_ref[s,at,:]=dot(ga,weights[s][:H,:],NT).astype(BF)
            so=squares(out,r); sm=squares(bm,r); sg=jnp.sum((gn*hat).reshape(R//8,8,D),axis=0)
            if r==0: sum_ref[0:8,:]=sg; sum_ref[8:16,:]=so; sum_ref[24:32,:]=sm
            else: sum_ref[0:8,:]+=sg; sum_ref[8:16,:]+=so; sum_ref[24:32,:]+=sm
        for s in range(n): go_ref[s]=dot(attn[s][...],g_s[...],TN).astype(BF)

def middle_part(scal,stream,cotangent,gain,attn,weights,tiles=2):
    n=len(attn); T,H=attn[0].shape; D=stream.shape[1]+1; FD=(weights[0].shape[0]-H)//2
    once=lambda a: pl.BlockSpec(a.shape,lambda i,sc:(0,)*a.ndim,pipeline_mode=pl.Buffered(1))
    whole=lambda *s: pl.BlockSpec(s,lambda i,sc:(0,)*len(s))
    return pl.pallas_call(
        functools.partial(middle_kernel,n,tiles),
        grid_spec=pltpu.PrefetchScalarGridSpec(num_scalar_prefetch=1,grid=(n,),
            in_specs=[once(stream),once(cotangent),once(gain)]+[once(a) for a in attn]+[once(w) for w in weights],
            out_specs=[whole(T,D-1),whole(T,D),whole(n,T,H),pl.BlockSpec((1,2*FD,D),lambda i,sc:(i,0,0)),whole(n,H,D),whole(32,D)],
            scratch_shapes=[pltpu.VMEM((T//tiles,D),F32),pltpu.VMEM((T,D),F32),pltpu.VMEM((T,D),BF),pltpu.VMEM((T,D),BF),pltpu.VMEM((T,D),F32),pltpu.VMEM((T,D),F32)]),
        out_shape=[jax.ShapeDtypeStruct((T,D-1),BF),jax.ShapeDtypeStruct((T,D),F32),jax.ShapeDtypeStruct((n,T,H),BF),
            jax.ShapeDtypeStruct((n,2*FD,D),BF),jax.ShapeDtypeStruct((n,H,D),BF),jax.ShapeDtypeStruct((32,D),F32)],
        compiler_params=pltpu.CompilerParams(vmem_limit_bytes=VMEM_LIMIT),
        name="middle",
    )(scal,stream,cotangent,gain,*attn,*weights)


def swap(x,axis,step):
    size=lax.axis_size(axis)
    return lax.ppermute(x,axis,[(i,i^step) for i in range(size)])

def after(x,*others):
    return lax.optimization_barrier((x,)+others)[0]

def gather_xor(x,axis):
    size=lax.axis_size(axis); got={0:x}
    step=size//2
    while step>=1:
        for have in sorted(got): got[have^step]=swap(got[have],axis,step)
        step//=2
    return [got[i] for i in range(size)]

def reduce_xor(pieces,axis):
    size=lax.axis_size(axis); step=1
    while step<size:
        keep=[i for i in sorted(pieces) if not i&step]
        sent=jnp.stack([pieces[i^step] for i in keep]) if len(keep)>1 else pieces[keep[0]^step][None]
        got=swap(sent.astype(BF),axis,step)
        if len(keep)==1: return pieces[0],got[0]
        pieces={i:pieces[i].astype(F32)+got[m].astype(F32) for m,i in enumerate(keep)}
        pieces={i:v.astype(BF) if i else v for i,v in pieces.items()}
        step*=2
    return pieces[0],None

def bit_groups(size):
    bits=[1<<b for b in range(size.bit_length()-1)]
    groups=[bits[:1]]; rest=bits[1:]
    while rest: groups.append(rest[:2]); rest=rest[2:]
    return [g for g in groups if g]

def sum_over(x,axis):
    me=lax.axis_index(axis); levels=[]
    cur=x.astype(F32)
    for bits in bit_groups(lax.axis_size(axis)):
        m=1<<len(bits); low=bits[0]
        mine=(me//low)%m
        cut=cur.reshape((m,cur.shape[0]//m)+cur.shape[1:])
        total=lax.dynamic_index_in_dim(cut,mine,0,keepdims=False)
        cutb=cut.astype(BF)
        for d in range(1,m):
            got=swap(lax.dynamic_index_in_dim(cutb,mine^d,0,keepdims=False),axis,d*low)
            total=total+got.astype(F32)
        levels.append((m,low,mine)); cur=total
    cur=cur.astype(BF)
    for m,low,mine in reversed(levels):
        full=jnp.zeros((m,)+cur.shape,BF)
        full=lax.dynamic_update_index_in_dim(full,cur,mine,0)
        for d in range(1,m):
            full=lax.dynamic_update_index_in_dim(full,swap(cur,axis,d*low),mine^d,0)
        cur=full.reshape((m*cur.shape[0],)+cur.shape[1:])
    return cur.astype(F32)

def butterfly(x,axis):
    step=1
    while step<lax.axis_size(axis):
        x=x+swap(x,axis,step); step*=2
    return x

def shards(stream,cotangent,bucket,row_counts,lengths,w_qkv,w_out,w_up,w_down,gain_one,gain_two):
    T=stream.shape[0]; D=stream.shape[1]+1; C=w_qkv.shape[2]; nh=C//HD
    n=lax.axis_size("tensor"); t=lax.axis_index("tensor")
    wide=-(-(C+4*nh)//LANES)*LANES
    span=BASE*jnp.where(bucket[0]==0,1,jnp.where(bucket[0]==1,2,4)).astype(jnp.int32)
    zero=jnp.zeros((),jnp.int32)
    scal=jnp.stack([t.astype(jnp.int32),span,row_counts[0]]+[lengths[0,r] for r in range(lengths.shape[1])]+[zero]*(13-lengths.shape[1])+[(t*T).astype(jnp.int32)])
    g1=gain_one.reshape(1,D); g2=gain_two.reshape(1,D)
    lift=np.ones((1,3,1),np.float32); lift[0,0]=HD**-0.5
    w_pad=jnp.pad(w_qkv*jnp.asarray(lift,BF),((0,0),(0,0),(0,wide-C))).reshape(D,3*wide)

    normed=first_norm(stream,g1)
    ones=gather_xor(normed,"tensor")
    gathered=jnp.concatenate(ones,axis=0)
    packed=dot(gathered,w_pad,NN).astype(BF)
    own_w=after(jnp.concatenate([w_out,w_up,w_down],axis=0),*ones)
    weights=gather_xor(own_w,"tensor")
    attn_all,qx=attn_fwd(scal,packed,T,nh)
    attn=[attn_all[:T]]+[swap(attn_all[d*T:(d+1)*T],"tensor",d) for d in range(1,n)]
    result,mid,grad_heads,gw,go,sums=middle_part(scal,stream,cotangent,g2,attn,weights)
    heads=jnp.concatenate([grad_heads[0]]+[swap(grad_heads[d],"tensor",d) for d in range(1,n)],axis=0)
    grad_packed=attn_bwd(scal,qx,packed,attn_all,heads,T,nh)

    gw,go=after(gw,go),go
    near,far=reduce_xor({i:gw[i] for i in range(n)},"tensor")
    near_o,far_o=reduce_xor({i:go[i] for i in range(n)},"tensor")
    gw_own=jnp.concatenate([near_o.astype(F32)+far_o.astype(F32),near.astype(F32)+far.astype(F32)],axis=0).astype(BF)
    gw_sum=lax.psum(gw_own,"dp").astype(F32)

    back=dot(grad_packed,w_pad,NT).astype(BF)
    own,far=reduce_xor({i:back[i*T:(i+1)*T] for i in range(n)},"tensor")
    grad_stream=last_norm(stream,mid,own,far,g1)
    gq=dot(gathered,grad_packed,TN)
    gq=gq.reshape(D,3,wide)[:,:,:C]*lift
    gain_part=jnp.sum(gq*w_qkv.astype(F32),axis=(1,2))/gain_one
    gq=sum_over(gq.reshape(D,3*C),"dp").reshape(D,3,C)
    group_tokens=jnp.sum(jnp.where(jnp.arange(lengths.shape[1])<row_counts[0],lengths[0],0)).astype(F32)/n
    s=sums.reshape(4,8,D)
    small=jnp.concatenate([gain_part,jnp.sum(s[0],axis=0),jnp.sum(s[1:],axis=(1,2)),group_tokens[None]])
    small=jnp.pad(small,(0,-small.shape[0]%LANES)).reshape(-1,LANES)
    small=butterfly(butterfly(small,"tensor"),"dp").reshape(-1)
    root=jnp.sqrt(small[2*D:2*D+3]/(D*small[2*D+3]))
    F=w_up.shape[1]
    return (result,grad_stream,gq,gw_sum[:C],gw_sum[C:C+D],gw_sum[C+D:],small[:D],small[D:2*D],root)


def solution(mesh):
    rows=P(("dp","tensor"),None)
    return jax.shard_map(shards,mesh=mesh,
        in_specs=(rows,rows,P("dp"),P("dp"),P("dp",None),P(None,None,"tensor"),P("tensor",None),P(None,"tensor"),P("tensor",None),P(),P()),
        out_specs=(rows,rows,P(None,None,"tensor"),P("tensor",None),P(None,"tensor"),P("tensor",None),P(),P(),P()),
        check_vma=False)
```

time: 1970 us -> 802 us (0.41)
  matrix products: 814 us -> 27.3 us
  waiting for transfers between devices: 590 us -> 193 us
  other arithmetic: 394 us -> 31.2 us
  Pallas kernels: 0 us -> 294 us
  starting transfers between devices: 0.37 us -> 179 us
  local copies, waits for them, and re-layouts: 106 us -> 56.5 us
  blocking collectives: 42 us -> 0 us
    dot_general x68 -> x3, matrix products: 814 us -> 27.3 us  [dot(): return lax.dot_general(a, b, dims, preferred_element_type=F32)]
    pallas_call x0 -> x5, Pallas kernels: none -> 294 us  [the longest x1 213 us: middle_part(): pl.pallas_call(functools.partial(middle_kernel, n, tiles), grid_spec=pltp...]
    reduce_scatter x4 -> x0, waiting for transfers between devices: 247 us -> none  [the longest x1 99.2 us: shards(): lax.psum_scatter(jnp.einsum('tf,df->td', grad_pre, w_up, preferred_elemen...]
    convert_element_type x17 -> x3, other arithmetic: 192 us -> 6.8 us  [the longest x2 6.75 us: reduce_xor(): pieces = {i: v.astype(BF) if i else v for i, v in pieces.items()}]
    ppermute x0 -> x31, starting transfers between devices: none -> 179 us  [swap(): return lax.ppermute(x, axis, [(i, i ^ step) for i in range(size)])]
    ppermute x0 -> x31, waiting for transfers between devices: none -> 166 us  [swap(): return lax.ppermute(x, axis, [(i, i ^ step) for i in range(size)])]
    psum x1, waiting for transfers between devices: 189 us -> 26.4 us  [shards(): gw_sum = lax.psum(gw_own, 'dp').astype(F32)]
    all_gather x4 -> x0, waiting for transfers between devices: 154 us -> none  [the longest x1 46.8 us: shards(): gathered_one = lax.all_gather(normed_one, 'tensor', axis=0, tiled=True)]
  transfers between devices with their start and end apart: 9 -> 32, of which waited for: 8 -> 14; matrix products, arithmetic and copies ran while one was open for 46% -> 12% of each run, Pallas kernels for 0% -> 10%
where the time goes in v1:
time: 802 us; the launch traced here: 798 us
  Pallas kernels  294 us (37%)
  waiting for transfers between devices  193 us (24%)
  starting transfers between devices  179 us (22%)
  local copies, waits for them, and re-layouts  56.5 us (7%)
  other arithmetic  31.2 us (4%)
  matrix products  27.3 us (3%)
  between operations  17.3 us (2%)
    pallas_call x1, Pallas kernels, middle_part(): pl.pallas_call(functools.partial(middle_kernel, n, tiles), grid_spec=pltp...  213 us
    ppermute x31, starting transfers between devices, swap(): return lax.ppermute(x, axis, [(i, i ^ step) for i in range(size)])  179 us
    ppermute x31, waiting for transfers between devices, swap(): return lax.ppermute(x, axis, [(i, i ^ step) for i in range(size)])  166 us
    pallas_call x1, Pallas kernels, attn_bwd(): pl.pallas_call(functools.partial(bwd_kernel, nh, bk, shard), grid_spec=pl...  42.3 us
    pallas_call x1, Pallas kernels, attn_fwd(): pl.pallas_call(functools.partial(fwd_kernel, nh, bq, shard), grid_spec=pl...  28.1 us
    dot_general x3, matrix products, dot(): return lax.dot_general(a, b, dims, preferred_element_type=F32)  27.3 us
    psum x1, waiting for transfers between devices, shards(): gw_sum = lax.psum(gw_own, 'dp').astype(F32)  26.4 us
  transfers between devices with their start and end apart: 32, of which 14 were waited for; matrix products, arithmetic and copies ran while one was open for 12% of the time, Pallas kernels for 10%

profile of v1, /device:TPU:0, one launch (start us, length us, event | category | flops | bytes accessed | tf_op | source)
XLA Modules:
  0.0 798.2 jit_solution(16115368757857124339)
XLA Ops:
  7.2 1.3 reshape.86.gain_ref
  8.5 4.0 first_norm.1
  12.6 3.0 collective-permute-start.1
  15.6 34.6 %collective-permute-done.1 = bf16[1024,768]{1,0:T(8,128)(2,1)S(1)} collective-permute-done((bf16[1024,768]{1,0:T(8,128)(2,1)}, bf16[1024,768]{1,0:T(8,128)(2,1)S(1)}, u32[]{:S(2)}, u32[]{:S(2)}) %collective-permute-start.1) | collective-permute-done | bytes 1572896 | tf_op jit(solution)/shard_map/ppermute | solution.py:360
  50.2 2.4 pad_maximum_fusion.3.refs_4_
  52.6 1.0 collective-permute-done.2
  53.6 1.7 collective-permute-start.7
  55.6 57.8 %collective-permute-done.7.refs_6_ = bf16[1728,768]{1,0:T(8,128)(2,1)} collective-permute-done((bf16[1728,768]{1,0:T(8,128)(2,1)S(1)}, bf16[1728,768]{1,0:T(8,128)(2,1)}, u32[]{:S(2)}, u32[]{:S(2)}) %collective-permute-start.7) | collective-permute-done | bytes 2654240 | tf_op jit(solution)/shard_map/ppermute | solution.py:360
  115.3 1.1 pad.8
  116.4 3.3 stack.27.sc_ref
  119.7 10.9 %convolution_convert_fusion.1.p_ref = bf16[4096,768]{1,0:T(8,128)(2,1)} fusion(bf16[768,768]{0,1:T(8,128)(2,1)} %bitcast.101, bf16[1024,768]{1,0:T(8,128)(2,1)} %copy-done.23, bf16[1024,768]{1,0:T(8,128)(2,1)} %copy-done.19, bf16[1024,768]{1,0:T(8,128)(2,1)} %copy-done.21, bf16[1024,768]{1,0:T(8,128)(2,1)} %first_norm.1), kind=kOutput, calls=%fused_computation.1 | convolution fusion | flops 4860149760 | bytes 13762560 | tf_op jit(solution)/shard_map/dot_general | solution.py:13
  130.5 28.1 %attention_forward.1 = (bf16[4096,192]{1,0:T(8,128)(2,1)}, bf16[4096,256]{1,0:T(8,128)(2,1)}) custom-call(s32[17]{0:T(128)} %stack.27.sc_ref, bf16[4096,768]{1,0:T(8,128)(2,1)} %convolution_convert_fusion.1.p_ref, bf16[8,256]{1,0:T(8,128)(2,1)} %constant.129.clone.mask_ref, bf16[256,128]{1,0:T(8,128)(2,1)} %constant.130.clone.fold_ref, ...), custom_call_target="tpu_custom_call" | custom-call | tf_op jit(solution)/shard_map/attention_forward/pallas_call | solution.py:131
  158.6 2.5 fusion.16
  161.6 1.7 collective-permute-start.4
  163.9 12.5 %collective-permute-done.4.refs_2_ = bf16[1024,192]{1,0:T(8,128)(2,1)S(1)} collective-permute-done((bf16[1024,192]{1,0:T(8,128)(2,1)S(1)}, bf16[1024,192]{1,0:T(8,128)(2,1)S(1)}, u32[]{:S(2)}, u32[]{:S(2)}) %collective-permute-start.4) | collective-permute-done | bytes 393248 | tf_op jit(solution)/shard_map/ppermute | solution.py:360
  176.4 9.5 %collective-permute-done.5.refs_3_ = bf16[1024,192]{1,0:T(8,128)(2,1)S(1)} collective-permute-done((bf16[1024,192]{1,0:T(8,128)(2,1)S(1)}, bf16[1024,192]{1,0:T(8,128)(2,1)S(1)}, u32[]{:S(2)}, u32[]{:S(2)}) %collective-permute-start.5) | collective-permute-done | bytes 393248 | tf_op jit(solution)/shard_map/ppermute | solution.py:360
  186.8 213.0 %middle.1 = (bf16[1024,767]{1,0:T(8,128)(2,1)}, f32[1024,768]{1,0:T(8,128)}, bf16[4,1024,192]{2,1,0:T(8,128)(2,1)}, bf16[4,1536,768]{2,1,0:T(8,128)(2,1)}, bf16[...) custom-call(s32[17]{0:T(128)} %stack.27.sc_ref, bf16[1024,767]{1,0:T(8,128)(2,1)} %x_ref.5, bf16[1024,767]{1,0:T(8,128)(2,1)} %c_ref.1, ...), custom_call_target="tpu_custom_call" | custom-call | tf_op jit(solution)/shard_map/middle/pallas_call | solution.py:345
  399.7 2.7 fusion.14
  402.4 2.5 pad_maximum_fusion.1
  406.9 1.1 slice_bitcast_fusion.7
  408.0 1.7 collective-permute-start.10
  410.3 1.1 fusion.17
  411.8 11.2 %collective-permute-done.10 = bf16[1024,192]{1,0:T(8,128)(2,1)S(1)} collective-permute-done((bf16[1024,192]{1,0:T(8,128)(2,1)}, bf16[1024,192]{1,0:T(8,128)(2,1)S(1)}, u32[]{:S(2)}, u32[]{:S(2)}) %collective-permute-start.10) | collective-permute-done | bytes 393248 | tf_op jit(solution)/shard_map/ppermute | solution.py:360
  423.0 9.6 %collective-permute-done.11 = bf16[1024,192]{1,0:T(8,128)(2,1)} collective-permute-done((bf16[1024,192]{1,0:T(8,128)(2,1)}, bf16[1024,192]{1,0:T(8,128)(2,1)}, u32[]{:S(2)}, u32[]{:S(2)}) %collective-permute-start.11) | collective-permute-done | bytes 393248 | tf_op jit(solution)/shard_map/ppermute | solution.py:360
  432.6 2.9 pad_maximum_fusion.5.g_ref
  435.5 42.3 %attention_backward.1 = bf16[4096,768]{1,0:T(8,128)(2,1)} custom-call(s32[17]{0:T(128)} %stack.27.sc_ref, bf16[4096,256]{1,0:T(8,128)(2,1)} %get-tuple-element.23.qx_ref, bf16[4096,768]{1,0:T(8,128)(2,1)} %convolution_convert_fusion.1.p_ref, bf16[4096,192]{1,0:T(8,128)(2,1)} %get-tuple-element.19.o_ref, bf16[4096,192]{1,0:T(8,128)(2,1)} %pad_maximum_fusion.5.g_ref, ...), custom_call_target="tpu_custom_call" | custom-call | tf_op jit(solution)/shard_map/attention_backward/pallas_call | solution.py:203
  477.8 8.4 %convolution_convert_fusion = bf16[4096,768]{1,0:T(8,128)(2,1)S(1)} fusion(bf16[4096,768]{1,0:T(8,128)(2,1)} %attention_backward.1, bf16[768,768]{0,1:T(8,128)(2,1)S(1)} %bitcast.102), kind=kOutput, calls=%fused_computation | convolution fusion | flops 4834983936 | bytes 13762560 | tf_op jit(solution)/shard_map/dot_general | solution.py:13
  486.4 3.0 copy-done.1
  489.4 1.9 pad_maximum_fusion.2
  491.9 4.8 add_convert_fusion.1
  496.7 1.8 collective-permute-start.25
  498.6 8.0 %fusion.3 = f32[768,768]{0,1:T(8,128)S(1)} fusion(bf16[4096,768]{1,0:T(8,128)(2,1)S(1)} %bitcast.95, bf16[1024,768]{1,0:T(8,128)(2,1)} %copy-done.23, bf16[1024,768]{1,0:T(8,128)(2,1)S(1)} %copy-done.20, bf16[1024,768]{1,0:T(8,128)(2,1)S(1)} %copy-done.22, bf16[1024,768]{1,0:T(8,128)(2,1)S(1)} %copy-done.5), kind=kOutput, calls=%fused_computation.21 | convolution fusion | flops 4857004032 | bytes 14942208 | tf_op jit(solution)/shard_map/dot_general | solution.py:13
  506.6 2.0 add_convert_fusion.3
  509.9 1.0 reshape_reshape.3
  511.8 30.8 %collective-permute-start.14 = (bf16[384,576]{0,1:T(8,128)(2,1)S(1)}, bf16[384,576]{0,1:T(8,128)(2,1)S(1)}, u32[]{:S(2)}, u32[]{:S(2)}) collective-permute-start(bf16[384,576]{0,1:T(8,128)(2,1)S(1)} %bitcast.104), channel_id=1, source_target_pairs={{0,4},{4,0},{8,12},{12,8},{16,20},{20,16},{24,28},{28,24},{1,5},{5... | collective-permute-start | bytes 1327112 | tf_op jit(solution)/shard_map/ppermute | solution.py:360
  542.6 13.7 %collective-permute-done.23 = bf16[1,192,768]{2,1,0:T(8,128)(2,1)} collective-permute-done((bf16[1,192,768]{2,1,0:T(8,128)(2,1)}, bf16[1,192,768]{2,1,0:T(8,128)(2,1)}, u32[]{:S(2)}, u32[]{:S(2)}) %collective-permute-start.23) | collective-permute-done | bytes 294944 | tf_op jit(solution)/shard_map/ppermute | solution.py:360
  556.3 1.2 fusion.4
  557.4 3.9 fusion.1
  561.4 1.8 pad_maximum_fusion.4
  564.0 1.8 collective-permute-start.27
  566.3 8.8 %collective-permute-start.15 = (bf16[96,576]{1,0:T(8,128)(2,1)S(1)}, bf16[96,576]{1,0:T(8,128)(2,1)S(1)}, u32[]{:S(2)}, u32[]{:S(2)}) collective-permute-start(bf16[96,576]{1,0:T(8,128)(2,1)S(1)} %get-tuple-element.51), channel_id=1, source_target_pairs={{0,8},{4,12},{8,0},{12,4},{16,24},{20,28},{24,16},{28,20},{1,9},{5... | collective-permute-start | bytes 331784 | tf_op jit(solution)/shard_map/ppermute | solution.py:360
  575.2 46.1 %collective-permute-start.16 = (bf16[96,576]{1,0:T(8,128)(2,1)S(1)}, bf16[96,576]{1,0:T(8,128)(2,1)S(1)}, u32[]{:S(2)}, u32[]{:S(2)}) collective-permute-start(bf16[96,576]{1,0:T(8,128)(2,1)S(1)} %get-tuple-element.53), channel_id=1, source_target_pairs={{0,16},{4,20},{8,24},{12,28},{16,0},{20,4},{24,8},{28,12},{1,17},{... | collective-permute-start | bytes 331784 | tf_op jit(solution)/shard_map/ppermute | solution.py:360
  621.3 1.4 collective-permute-start.17
  622.7 5.7 fusion.2
  628.8 2.4 collective-permute-done.17
  631.3 2.2 collective-permute-start.18
  633.5 54.7 %collective-permute-start.28 = (f32[13,128]{1,0:T(8,128)S(1)}, f32[13,128]{1,0:T(8,128)S(1)}, u32[]{:S(2)}, u32[]{:S(2)}) collective-permute-start(f32[13,128]{1,0:T(8,128)S(1)} %fusion.23), channel_id=1, source_target_pairs={{0,4},{4,0},{8,12},{12,8},{16,20},{20,16},{24,28},{28,24},{1,5},{5... | collective-permute-start | bytes 19976 | tf_op jit(solution)/shard_map/ppermute | solution.py:360
  688.3 1.6 collective-permute-done.28
  689.9 3.7 collective-permute-done.29
  693.6 2.2 collective-permute-start.30
  695.8 2.3 collective-permute-done.30
  699.4 2.3 collective-permute-start.19
  701.7 1.5 collective-permute-start.20
  703.2 6.4 collective-permute-done.19
  709.7 13.7 %collective-permute-start.21 = (bf16[384,576]{1,0:T(8,128)(2,1)S(1)}, bf16[384,576]{1,0:T(8,128)(2,1)S(1)}, u32[]{:S(2)}, u32[]{:S(2)}) collective-permute-start(bf16[384,576]{1,0:T(8,128)(2,1)S(1)} %bitcast.98), channel_id=1, source_target_pairs={{0,4},{4,0},{8,12},{12,8},{16,20},{20,16},{24,28},{28,24},{1,5},{5... | collective-permute-start | bytes 1327112 | tf_op jit(solution)/shard_map/ppermute | solution.py:360
  724.5 1.2 copy.35
  726.2 11.3 %dynamic_update_slice.24 = bf16[2,384,576]{1,0,2:T(2,128)(2,1)S(1)} dynamic-update-slice(bf16[2,384,576]{1,0,2:T(2,128)(2,1)S(1)} %broadcast_in_dim.39, bf16[1,384,576]{1,0,2:T(2,128)(2,1)S(1)} %copy.35, s32[]{:T(128)S(6)} %select_n.63, s32[]{:T(128)} %constant.115.clone.1, s32[]{:T(128)} %constant.115.clone.1) | dynamic-update-slice | bytes 884740 | tf_op jit(solution)/shard_map/jit(dynamic_update_index_in_dim)/dynamic_update_slice | solution.py:407
  737.5 1.2 copy.37
  738.8 11.3 %dynamic_update_slice.25 = bf16[2,384,576]{1,0,2:T(2,128)(2,1)S(1)} dynamic-update-slice(bf16[2,384,576]{1,0,2:T(2,128)(2,1)S(1)} %dynamic_update_slice.24, bf16[1,384,576]{1,0,2:T(2,128)(2,1)S(1)} %copy.37, s32[]{:T(128)S(6)} %select_n.64, s32[]{:T(128)} %constant.115.clone.1, s32[]{:T(128)} %constant.115.clone.1) | dynamic-update-slice | bytes 884740 | tf_op jit(solution)/shard_map/jit(dynamic_update_index_in_dim)/dynamic_update_slice | solution.py:409
  750.1 1.7 reshape.95
  751.8 7.0 last_norm.1
  758.8 26.4 %all-reduce.4.cloned.1.call-done = bf16[1728,768]{1,0:T(8,128)(2,1)} async-done(((bf16[1728,768]{1,0:T(8,128)(2,1)}), bf16[1728,768]{1,0:T(8,128)(2,1)}) %all-reduce.4.cloned.1.call-update) | async-done | bytes 2654224 | tf_op jit(solution)/shard_map/psum | solution.py:446
  785.2 4.2 fusion.15
  789.4 1.8 slice.181
  (123 shorter events, 12.2 us)
Async XLA Ops:
  7.2 43.0 %copy-start.12 = (bf16[192,768]{1,0:T(8,128)(2,1)S(1)}, bf16[192,768]{1,0:T(8,128)(2,1)}, u32[]{:S(2)}) copy-start(bf16[192,768]{1,0:T(8,128)(2,1)} %param.24) | copy-start | bytes 884740
  7.2 778.0 %all-reduce.4.cloned.1.call-start = ((), (), s32[]{:S(2)}) async-start(), calls=%async_computation | async-start | bytes 5308416 | tf_op jit(solution)/shard_map/psum | solution.py:446
  12.6 42.8 %copy-start.2 = (bf16[768,3,192]{0,2,1:T(8,128)(2,1)S(1)}, bf16[768,3,192]{0,2,1:T(8,128)(2,1)}, u32[]{:S(2)}) copy-start(bf16[768,3,192]{0,2,1:T(8,128)(2,1)} %param.23) | copy-start | bytes 2654212
  12.6 42.8 %copy-start.17 = (bf16[3]{0:T(256)(128)(2,1)S(1)}, bf16[3]{0:T(256)(128)(2,1)}, u32[]{:S(2)}) copy-start(bf16[3]{0:T(256)(128)(2,1)} %constant.140) | copy-start | bytes 22
  12.6 100.8 %copy-start.15 = (s32[1,4]{1,0:T(1,128)S(1)}, s32[1,4]{1,0:T(1,128)}, u32[]{:S(2)}) copy-start(s32[1,4]{1,0:T(1,128)} %param.22) | copy-start | bytes 52
  12.6 37.6 %collective-permute-start.1 = (bf16[1024,768]{1,0:T(8,128)(2,1)}, bf16[1024,768]{1,0:T(8,128)(2,1)S(1)}, u32[]{:S(2)}, u32[]{:S(2)}) collective-permute-start(bf16[1024,768]{1,0:T(8,128)(2,1)} %first_norm.1), channel_id=1, source_target_pairs={{0,2},{1,3},{2,0},{3,1},{4,6},{5,7},{6,4},{7,5},{8,10},{9,11},{10,... | collective-permute-start | bytes 4718600 | tf_op jit(solution)/shard_map/ppermute | solution.py:360
  15.6 37.0 %collective-permute-start = (bf16[1024,768]{1,0:T(8,128)(2,1)}, bf16[1024,768]{1,0:T(8,128)(2,1)S(1)}, u32[]{:S(2)}, u32[]{:S(2)}) collective-permute-start(bf16[1024,768]{1,0:T(8,128)(2,1)} %first_norm.1), channel_id=1, source_target_pairs={{0,1},{1,0},{2,3},{3,2},{4,5},{5,4},{6,7},{7,6},{8,9},{9,8},{10,11... | collective-permute-start | bytes 4718600 | tf_op jit(solution)/shard_map/ppermute | solution.py:360
  50.2 2.4 copy-start.19
  50.2 3.4 collective-permute-start.2
  52.6 77.9 %copy-start = (bf16[1728,768]{1,0:T(8,128)(2,1)}, bf16[1728,768]{1,0:T(8,128)(2,1)S(1)}, u32[]{:S(2)}) copy-start(bf16[1728,768]{1,0:T(8,128)(2,1)S(1)} %pad_maximum_fusion.3.refs_4_) | copy-start | bytes 7962628
  52.6 60.7 %copy-start.21 = (bf16[1024,768]{1,0:T(8,128)(2,1)}, bf16[1024,768]{1,0:T(8,128)(2,1)S(1)}, u32[]{:S(2)}) copy-start(bf16[1024,768]{1,0:T(8,128)(2,1)S(1)} %collective-permute-done) | copy-start | bytes 4718596
  53.6 59.7 %copy-start.23 = (bf16[1024,768]{1,0:T(8,128)(2,1)}, bf16[1024,768]{1,0:T(8,128)(2,1)S(1)}, u32[]{:S(2)}) copy-start(bf16[1024,768]{1,0:T(8,128)(2,1)S(1)} %collective-permute-done.2) | copy-start | bytes 4718596
  53.6 59.7 %collective-permute-start.7 = (bf16[1728,768]{1,0:T(8,128)(2,1)S(1)}, bf16[1728,768]{1,0:T(8,128)(2,1)}, u32[]{:S(2)}, u32[]{:S(2)}) collective-permute-start(bf16[1728,768]{1,0:T(8,128)(2,1)S(1)} %pad_maximum_fusion.3.refs_4_), channel_id=1, source_target_pairs={{0,2},{1,3},{2,0},{3,1},{4,6},{5,7},{6,4},{7,5},{8,10},{9,11},{10,... | collective-permute-start | bytes 7962632 | tf_op jit(solution)/shard_map/ppermute | solution.py:360
  55.5 130.4 %collective-permute-start.6 = (bf16[1728,768]{1,0:T(8,128)(2,1)S(1)}, bf16[1728,768]{1,0:T(8,128)(2,1)}, u32[]{:S(2)}, u32[]{:S(2)}) collective-permute-start(bf16[1728,768]{1,0:T(8,128)(2,1)S(1)} %pad_maximum_fusion.3.refs_4_), channel_id=1, source_target_pairs={{0,1},{1,0},{2,3},{3,2},{4,5},{5,4},{6,7},{7,6},{8,9},{9,8},{10,11... | collective-permute-start | bytes 7962632 | tf_op jit(solution)/shard_map/ppermute | solution.py:360
  113.3 73.4 %collective-permute-start.8 = (bf16[1728,768]{1,0:T(8,128)(2,1)}, bf16[1728,768]{1,0:T(8,128)(2,1)}, u32[]{:S(2)}, u32[]{:S(2)}) collective-permute-start(bf16[1728,768]{1,0:T(8,128)(2,1)} %collective-permute-done.7.refs_6_), channel_id=1, source_target_pairs={{0,1},{1,0},{2,3},{3,2},{4,5},{5,4},{6,7},{7,6},{8,9},{9,8},{10,11... | collective-permute-start | bytes 7962632 | tf_op jit(solution)/shard_map/ppermute | solution.py:360
  158.6 4.7 copy-start.16
  161.1 2.8 collective-permute-start.3
  161.6 14.8 %collective-permute-start.4 = (bf16[1024,192]{1,0:T(8,128)(2,1)S(1)}, bf16[1024,192]{1,0:T(8,128)(2,1)S(1)}, u32[]{:S(2)}, u32[]{:S(2)}) collective-permute-start(bf16[1024,192]{1,0:T(8,128)(2,1)S(1)} %get-tuple-element.46), channel_id=1, source_target_pairs={{0,2},{1,3},{2,0},{3,1},{4,6},{5,7},{6,4},{7,5},{8,10},{9,11},{10,... | collective-permute-start | bytes 1179656 | tf_op jit(solution)/shard_map/ppermute | solution.py:360
  163.3 22.6 %collective-permute-start.5 = (bf16[1024,192]{1,0:T(8,128)(2,1)S(1)}, bf16[1024,192]{1,0:T(8,128)(2,1)S(1)}, u32[]{:S(2)}, u32[]{:S(2)}) collective-permute-start(bf16[1024,192]{1,0:T(8,128)(2,1)S(1)} %get-tuple-element.45), channel_id=1, source_target_pairs={{0,3},{1,2},{2,1},{3,0},{4,7},{5,6},{6,5},{7,4},{8,11},{9,10},{10,... | collective-permute-start | bytes 1179656 | tf_op jit(solution)/shard_map/ppermute | solution.py:360
  163.9 22.8 %copy-start.9 = (bf16[1024,192]{1,0:T(8,128)(2,1)}, bf16[1024,192]{1,0:T(8,128)(2,1)S(1)}, u32[]{:S(2)}) copy-start(bf16[1024,192]{1,0:T(8,128)(2,1)S(1)} %collective-permute-done.3.refs_1_) | copy-start | bytes 1179652
  176.4 10.4 %copy-start.10 = (bf16[1024,192]{1,0:T(8,128)(2,1)}, bf16[1024,192]{1,0:T(8,128)(2,1)S(1)}, u32[]{:S(2)}) copy-start(bf16[1024,192]{1,0:T(8,128)(2,1)S(1)} %collective-permute-done.4.refs_2_) | copy-start | bytes 1179652
  185.9 0.8 copy-start.11
  402.4 4.4 copy-start.4
  405.0 5.1 copy-start.13
  405.0 86.9 %collective-permute-start.24 = (bf16[2,1536,768]{2,1,0:T(8,128)(2,1)}, bf16[2,1536,768]{2,1,0:T(8,128)(2,1)}, u32[]{:S(2)}, u32[]{:S(2)}) collective-permute-start(bf16[2,1536,768]{2,1,0:T(8,128)(2,1)} %pad_maximum_fusion.1), channel_id=1, source_target_pairs={{0,1},{1,0},{2,3},{3,2},{4,5},{5,4},{6,7},{7,6},{8,9},{9,8},{10,11... | collective-permute-start | bytes 14155784 | tf_op jit(solution)/shard_map/ppermute | solution.py:360
  408.0 15.0 %collective-permute-start.10 = (bf16[1024,192]{1,0:T(8,128)(2,1)}, bf16[1024,192]{1,0:T(8,128)(2,1)S(1)}, u32[]{:S(2)}, u32[]{:S(2)}) collective-permute-start(bf16[1024,192]{1,0:T(8,128)(2,1)} %get-tuple-element.43), channel_id=1, source_target_pairs={{0,2},{1,3},{2,0},{3,1},{4,6},{5,7},{6,4},{7,5},{8,10},{9,11},{10,... | collective-permute-start | bytes 1179656 | tf_op jit(solution)/shard_map/ppermute | solution.py:360
  409.7 22.9 %collective-permute-start.11 = (bf16[1024,192]{1,0:T(8,128)(2,1)}, bf16[1024,192]{1,0:T(8,128)(2,1)}, u32[]{:S(2)}, u32[]{:S(2)}) collective-permute-start(bf16[1024,192]{1,0:T(8,128)(2,1)} %get-tuple-element.42), channel_id=1, source_target_pairs={{0,3},{1,2},{2,1},{3,0},{4,7},{5,6},{6,5},{7,4},{8,11},{9,10},{10,... | collective-permute-start | bytes 1179656 | tf_op jit(solution)/shard_map/ppermute | solution.py:360
  409.7 22.9 %collective-permute-start.9 = (bf16[1024,192]{1,0:T(8,128)(2,1)S(1)}, bf16[1024,192]{1,0:T(8,128)(2,1)}, u32[]{:S(2)}, u32[]{:S(2)}) collective-permute-start(bf16[1024,192]{1,0:T(8,128)(2,1)S(1)} %get-tuple-element.44), channel_id=1, source_target_pairs={{0,1},{1,0},{2,3},{3,2},{4,5},{5,4},{6,7},{7,6},{8,9},{9,8},{10,11... | collective-permute-start | bytes 1179656 | tf_op jit(solution)/shard_map/ppermute | solution.py:360
  411.5 95.1 %collective-permute-start.22 = (bf16[2,192,768]{2,1,0:T(8,128)(2,1)S(1)}, bf16[2,192,768]{2,1,0:T(8,128)(2,1)S(1)}, u32[]{:S(2)}, u32[]{:S(2)}) collective-permute-start(bf16[2,192,768]{2,1,0:T(8,128)(2,1)S(1)} %pad_maximum_fusion.8), channel_id=1, source_target_pairs={{0,1},{1,0},{2,3},{3,2},{4,5},{5,4},{6,7},{7,6},{8,9},{9,8},{10,11... | collective-permute-start | bytes 1769480 | tf_op jit(solution)/shard_map/ppermute | solution.py:360
  435.5 42.3 %copy-start.6 = (bf16[768,3,256]{0,2,1:T(8,128)(2,1)S(1)}, bf16[768,3,256]{0,2,1:T(8,128)(2,1)}, u32[]{:S(2)}) copy-start(bf16[768,3,256]{0,2,1:T(8,128)(2,1)} %pad.8) | copy-start | bytes 3538948
  486.2 3.2 copy-start.1
  486.2 12.3 %slice-start = ((s8[6291456]{0:T(1024)(128)(4,1)}), s8[4194304]{0:T(1024)(128)(4,1)S(1)}, s32[]{:S(2)}) async-start(s8[6291456]{0:T(1024)(128)(4,1)} %bitcast.94), calls=%async_computation.1 | async-start | bytes 8388608
  489.4 9.1 %slice-start.1 = ((s8[6291456]{0:T(1024)(128)(4,1)}), s8[2097152]{0:T(1024)(128)(4,1)S(1)}, s32[]{:S(2)}) async-start(s8[6291456]{0:T(1024)(128)(4,1)} %bitcast.94), calls=%async_computation.2 | async-start | bytes 4194304
  491.3 7.2 copy-start.5
  491.3 7.2 copy-start.20
  491.3 7.2 copy-start.22
  491.3 131.3 %collective-permute-start.12 = (bf16[2,1024,768]{2,1,0:T(8,128)(2,1)}, bf16[2,1024,768]{2,1,0:T(8,128)(2,1)}, u32[]{:S(2)}, u32[]{:S(2)}) collective-permute-start(bf16[2,1024,768]{2,1,0:T(8,128)(2,1)} %pad_maximum_fusion.2), channel_id=1, source_target_pairs={{0,1},{1,0},{2,3},{3,2},{4,5},{5,4},{6,7},{7,6},{8,9},{9,8},{10,11... | collective-permute-start | bytes 9437192 | tf_op jit(solution)/shard_map/ppermute | solution.py:360
  496.7 12.1 %copy-start.3 = (bf16[768,3,192]{0,2,1:T(8,128)(2,1)S(1)}, bf16[768,3,192]{0,2,1:T(8,128)(2,1)}, u32[]{:S(2)}) copy-start(bf16[768,3,192]{0,2,1:T(8,128)(2,1)} %param.23) | copy-start | bytes 2654212
  496.7 12.1 %copy-start.18 = (f32[3]{0:T(128)S(1)}, f32[3]{0:T(128)}, u32[]{:S(2)}) copy-start(f32[3]{0:T(128)} %constant.141) | copy-start | bytes 40
  496.7 60.7 %collective-permute-start.25 = (bf16[1,1536,768]{2,1,0:T(8,128)(2,1)}, bf16[1,1536,768]{2,1,0:T(8,128)(2,1)}, u32[]{:S(2)}, u32[]{:S(2)}) collective-permute-start(bf16[1,1536,768]{2,1,0:T(8,128)(2,1)} %add_convert_fusion.1), channel_id=1, source_target_pairs={{0,2},{1,3},{2,0},{3,1},{4,6},{5,7},{6,4},{7,5},{8,10},{9,11},{10,... | collective-permute-start | bytes 7077896 | tf_op jit(solution)/shard_map/ppermute | solution.py:360
  506.6 2.6 copy-start.14
  506.6 2.6 copy-start.7
  508.6 47.7 %collective-permute-start.23 = (bf16[1,192,768]{2,1,0:T(8,128)(2,1)}, bf16[1,192,768]{2,1,0:T(8,128)(2,1)}, u32[]{:S(2)}, u32[]{:S(2)}) collective-permute-start(bf16[1,192,768]{2,1,0:T(8,128)(2,1)} %add_convert_fusion.3), channel_id=1, source_target_pairs={{0,2},{1,3},{2,0},{3,1},{4,6},{5,7},{6,4},{7,5},{8,10},{9,11},{10,... | collective-permute-start | bytes 884744 | tf_op jit(solution)/shard_map/ppermute | solution.py:360
  509.9 54.0 %collective-permute-start.26 = (f32[13,128]{1,0:T(8,128)}, f32[13,128]{1,0:T(8,128)S(1)}, u32[]{:S(2)}, u32[]{:S(2)}) collective-permute-start(f32[13,128]{1,0:T(8,128)} %pad_bitcast_fusion), channel_id=1, source_target_pairs={{0,1},{1,0},{2,3},{3,2},{4,5},{5,4},{6,7},{7,6},{8,9},{9,8},{10,11... | collective-permute-start | bytes 19976 | tf_op jit(solution)/shard_map/ppermute | solution.py:360
  510.9 45.4 %copy-start.8 = (bf16[2,192,768]{2,1,0:T(8,128)(2,1)S(1)}, bf16[2,192,768]{2,1,0:T(8,128)(2,1)}, u32[]{:S(2)}) copy-start(bf16[2,192,768]{2,1,0:T(8,128)(2,1)} %copy-done.7) | copy-start | bytes 1769476
  511.8 54.0 %collective-permute-start.14 = (bf16[384,576]{0,1:T(8,128)(2,1)S(1)}, bf16[384,576]{0,1:T(8,128)(2,1)S(1)}, u32[]{:S(2)}, u32[]{:S(2)}) collective-permute-start(bf16[384,576]{0,1:T(8,128)(2,1)S(1)} %bitcast.104), channel_id=1, source_target_pairs={{0,4},{4,0},{8,12},{12,8},{16,20},{20,16},{24,28},{28,24},{1,5},{5... | collective-permute-start | bytes 1327112 | tf_op jit(solution)/shard_map/ppermute | solution.py:360
  564.0 69.5 %collective-permute-start.27 = (f32[13,128]{1,0:T(8,128)S(1)}, f32[13,128]{1,0:T(8,128)S(1)}, u32[]{:S(2)}, u32[]{:S(2)}) collective-permute-start(f32[13,128]{1,0:T(8,128)S(1)} %fusion.12), channel_id=1, source_target_pairs={{0,2},{1,3},{2,0},{3,1},{4,6},{5,7},{6,4},{7,5},{8,10},{9,11},{10,... | collective-permute-start | bytes 19976 | tf_op jit(solution)/shard_map/ppermute | solution.py:360
  566.3 62.5 %collective-permute-start.15 = (bf16[96,576]{1,0:T(8,128)(2,1)S(1)}, bf16[96,576]{1,0:T(8,128)(2,1)S(1)}, u32[]{:S(2)}, u32[]{:S(2)}) collective-permute-start(bf16[96,576]{1,0:T(8,128)(2,1)S(1)} %get-tuple-element.51), channel_id=1, source_target_pairs={{0,8},{4,12},{8,0},{12,4},{16,24},{20,28},{24,16},{28,20},{1,9},{5... | collective-permute-start | bytes 331784 | tf_op jit(solution)/shard_map/ppermute | solution.py:360
  575.2 53.6 %collective-permute-start.16 = (bf16[96,576]{1,0:T(8,128)(2,1)S(1)}, bf16[96,576]{1,0:T(8,128)(2,1)S(1)}, u32[]{:S(2)}, u32[]{:S(2)}) collective-permute-start(bf16[96,576]{1,0:T(8,128)(2,1)S(1)} %get-tuple-element.53), channel_id=1, source_target_pairs={{0,16},{4,20},{8,24},{12,28},{16,0},{20,4},{24,8},{28,12},{1,17},{... | collective-permute-start | bytes 331784 | tf_op jit(solution)/shard_map/ppermute | solution.py:360
  621.3 9.9 %collective-permute-start.17 = (bf16[96,576]{1,0:T(8,128)(2,1)S(1)}, bf16[96,576]{1,0:T(8,128)(2,1)S(1)}, u32[]{:S(2)}, u32[]{:S(2)}) collective-permute-start(bf16[96,576]{1,0:T(8,128)(2,1)S(1)} %get-tuple-element.52), channel_id=1, source_target_pairs={{0,24},{4,28},{8,16},{12,20},{16,8},{20,12},{24,0},{28,4},{1,25},{... | collective-permute-start | bytes 331784 | tf_op jit(solution)/shard_map/ppermute | solution.py:360
  628.3 123.4 %collective-permute-start.13 = (bf16[1,1024,768]{2,1,0:T(8,128)(2,1)}, bf16[1,1024,768]{2,1,0:T(8,128)(2,1)}, u32[]{:S(2)}, u32[]{:S(2)}) collective-permute-start(bf16[1,1024,768]{2,1,0:T(8,128)(2,1)} %get-tuple-element.33), channel_id=1, source_target_pairs={{0,2},{1,3},{2,0},{3,1},{4,6},{5,7},{6,4},{7,5},{8,10},{9,11},{10,... | collective-permute-start | bytes 4718600 | tf_op jit(solution)/shard_map/ppermute | solution.py:360
  631.3 71.9 %collective-permute-start.18 = (bf16[96,576]{1,0:T(8,128)(2,1)S(1)}, bf16[96,576]{1,0:T(8,128)(2,1)S(1)}, u32[]{:S(2)}, u32[]{:S(2)}) collective-permute-start(bf16[96,576]{1,0:T(8,128)(2,1)S(1)} %get-tuple-element.30), channel_id=1, source_target_pairs={{0,8},{4,12},{8,0},{12,4},{16,24},{20,28},{24,16},{28,20},{1,9},{5... | collective-permute-start | bytes 331784 | tf_op jit(solution)/shard_map/ppermute | solution.py:360
  633.5 56.4 %collective-permute-start.28 = (f32[13,128]{1,0:T(8,128)S(1)}, f32[13,128]{1,0:T(8,128)S(1)}, u32[]{:S(2)}, u32[]{:S(2)}) collective-permute-start(f32[13,128]{1,0:T(8,128)S(1)} %fusion.23), channel_id=1, source_target_pairs={{0,4},{4,0},{8,12},{12,8},{16,20},{20,16},{24,28},{28,24},{1,5},{5... | collective-permute-start | bytes 19976 | tf_op jit(solution)/shard_map/ppermute | solution.py:360
  689.9 3.7 collective-permute-start.29
  693.6 4.5 collective-permute-start.30
  699.4 10.2 %collective-permute-start.19 = (bf16[96,576]{1,0:T(8,128)(2,1)S(1)}, bf16[96,576]{1,0:T(8,128)(2,1)S(1)}, u32[]{:S(2)}, u32[]{:S(2)}) collective-permute-start(bf16[96,576]{1,0:T(8,128)(2,1)S(1)} %get-tuple-element.30), channel_id=1, source_target_pairs={{0,16},{4,20},{8,24},{12,28},{16,0},{20,4},{24,8},{28,12},{1,17},{... | collective-permute-start | bytes 331784 | tf_op jit(solution)/shard_map/ppermute | solution.py:360
  701.7 8.0 collective-permute-start.20
  709.7 27.8 %collective-permute-start.21 = (bf16[384,576]{1,0:T(8,128)(2,1)S(1)}, bf16[384,576]{1,0:T(8,128)(2,1)S(1)}, u32[]{:S(2)}, u32[]{:S(2)}) collective-permute-start(bf16[384,576]{1,0:T(8,128)(2,1)S(1)} %bitcast.98), channel_id=1, source_target_pairs={{0,4},{4,0},{8,12},{12,8},{16,20},{20,16},{24,28},{28,24},{1,5},{5... | collective-permute-start | bytes 1327112 | tf_op jit(solution)/shard_map/ppermute | solution.py:360
Sparse Core Ops, SparseCore 0:
  563.3 221.8 all-reduce.3

commit v2 on v1

v2 whole, which is shorter than its diff:
```python
import functools
import jax, jax.numpy as jnp, numpy as np
from jax import lax
from jax.experimental import pallas as pl
from jax.experimental.pallas import tpu as pltpu
from jax.sharding import PartitionSpec as P
HD=64; BASE=1024
LANES=128
SHIFT_LIMIT=70.0
F32=jnp.float32; BF=jnp.bfloat16
NT=(((1,),(1,)),((),()))
NN=(((1,),(0,)),((),()))
def dot(a,b,dims): return lax.dot_general(a,b,dims,preferred_element_type=F32)

def tables(nh, wide):
    cols=nh*HD; lane=np.arange(wide)
    head=np.where(lane<cols,lane//HD,np.where(lane<cols+4*nh,(lane-cols)//4,-1))
    spare=(lane>=cols)&(lane<cols+4*nh)
    masks=np.zeros((8,wide),np.float32)
    for h in range(nh): masks[h]=(head==h)
    masks[nh]=spare
    for h in range(nh): masks[nh+1+h]=spare&(head==h)
    fold=np.zeros((wide,LANES),np.float32)
    hi=wide-LANES
    same=(head[:,None]==head[None,hi:])&(head[:,None]>=0)
    fold[:]=same&(lane<cols)[:,None]&spare[None,hi:]
    spread=np.zeros((LANES,wide),np.float32)
    spread[:]=(same&(lane<cols)[:,None]&spare[None,hi:]).T
    return jnp.asarray(masks,BF),jnp.asarray(fold,BF),jnp.asarray(spread,BF)

def row_info(sc_ref, start):
    span=sc_ref[1]
    row=start//span
    length=sc_ref[3]
    for r in range(1,4):
        length=jnp.where(row==r, sc_ref[3+r], length)
    length=jnp.where(row<sc_ref[2], length, 0)
    return row*span, row*span+length, row*span+span

def place(sc_ref, start, shard):
    return pl.multiple_of((jnp.bitwise_xor(start//shard, sc_ref[0]))*shard + start%shard, 256)

def parts(x, cols, hi):
    lane=lax.broadcasted_iota(jnp.int32,x.shape,1)+hi-cols
    which=jnp.where(lane<0,3,lane%4)
    a=x.astype(BF).astype(F32); r=x-a; b=r.astype(BF).astype(F32); c=r-b
    return jnp.where(which==0,a,jnp.where(which==1,b,jnp.where(which==2,c,0.0))).astype(BF)

def fwd_kernel(nh, bq, shard, sc_ref, p_ref, mask_ref, fold_ref, spread_ref, *refs):
    n=p_ref.shape[0]//shard; o_refs=refs[:n]; qx_ref, q_s, k_s, v_s, kn_s, sh_s, a_s=refs[n:]
    T=p_ref.shape[0]; W=p_ref.shape[1]//3; hi=W-LANES; cols=nh*HD
    i=pl.program_id(0)
    @pl.when(i==0)
    def _():
        kn=jnp.zeros((8,LANES),F32)
        for c in range(0,T,512):
            k=p_ref[c:c+512,W:2*W]; v=p_ref[c:c+512,2*W:]
            k_s[c:c+512,:]=k+mask_ref[nh:nh+1,:]
            kn=jnp.maximum(kn,jnp.max(dot(k*k,fold_ref[...],NN).reshape(64,8,LANES),axis=0))
            for h in range(nh):
                v_s[h,c:c+512,:]=v*mask_ref[h:h+1,:]+mask_ref[nh+1+h:nh+2+h,:]
        kn_s[...]=jnp.broadcast_to(jnp.max(kn,axis=0,keepdims=True),(8,LANES))
    start=i*bq
    row_start,valid_end,_=row_info(sc_ref,start)
    at=place(sc_ref,start,shard)
    q=p_ref[pl.ds(at,bq),:W]; own=p_ref[pl.ds(at,bq),W:2*W]
    before=(start-row_start)//bq
    full=jnp.minimum(before,(valid_end-row_start)//bq)
    some=jnp.minimum(before,(valid_end-row_start+bq-1)//bq)
    rows=lax.broadcasted_iota(jnp.int32,(bq,bq),0); tcol=lax.broadcasted_iota(jnp.int32,(bq,bq),1)
    diag=(tcol==rows)|((tcol<rows)&(tcol<valid_end-start))
    def set_q(shift_lanes):
        x=jnp.concatenate([q[:,:hi],q[:,hi:]+shift_lanes],axis=1)
        for h in range(nh): q_s[h]=x*mask_ref[h:h+1,:]
    self_score=dot(q*own,fold_ref[...],NN)
    shift=self_score.astype(BF).astype(F32)
    sh_s[...]=shift
    set_q(parts(-shift,cols,hi))
    size=jnp.sqrt(dot(q*q,fold_ref[...],NN)*kn_s[:1,:])*1.02
    bounded=jnp.max(size-shift)<=SHIFT_LIMIT
    @pl.when(jnp.logical_not(bounded))
    def _():
        lane=lax.broadcasted_iota(jnp.int32,(bq,LANES),1)+hi-cols
        new=jnp.zeros((bq,LANES),F32)
        for h in range(nh):
            qh=q*mask_ref[h:h+1,:]
            m0=jnp.max(jnp.where(diag,dot(qh,k_s[pl.ds(at,bq),:],NT),-1e30),axis=1,keepdims=True)
            def look(j,m):
                b=row_start+j*bq
                s=dot(qh,k_s[pl.ds(place(sc_ref,b,shard),bq),:],NT)
                s=jnp.where(tcol<valid_end-b,s,-1e30)
                return jnp.maximum(m,jnp.max(s,axis=1,keepdims=True))
            m=lax.fori_loop(0,some,look,m0)
            new=jnp.where((lane>=4*h)&(lane<4*h+4),m,new)
        sh_s[...]=new
        set_q(parts(-new,cols,hi))
    def step(b,masking,first):
        bt=place(sc_ref,b,shard)
        k=k_s[pl.ds(bt,bq),:]
        ps=[]
        for h in range(nh):
            s=dot(q_s[h],k,NT)
            if masking is not None: s=jnp.where(masking,s,-1e30)
            ps.append(jnp.exp(s).astype(BF))
        new=dot(jnp.concatenate(ps,axis=1),v_s[:,pl.ds(bt,bq),:].reshape(nh*bq,W),NN)
        if first: a_s[...]=new
        else: a_s[...]+=new
    step(start,diag,True)
    def whole(j,c):
        step(row_start+j*bq,None,False); return c
    def partly(j,c):
        b=row_start+j*bq
        step(b,tcol<valid_end-b,False); return c
    lax.fori_loop(0,full,whole,0)
    lax.fori_loop(full,some,partly,0)
    total=a_s[:,hi:]
    lane=lax.broadcasted_iota(jnp.int32,(bq,LANES),1)+hi-cols
    spare=(lane>=0)&(lane<4*nh)
    total=jnp.where(spare,total,1.0)
    out=(a_s[:,:cols]*dot(parts(1.0/total,cols,hi),spread_ref[...],NN)[:,:cols]).astype(BF)
    for s in range(n):
        @pl.when(at//shard==s)
        def _(): o_refs[s][pl.ds(pl.multiple_of(at%shard,bq),bq),:]=out
    lse=jnp.where(spare,sh_s[...]+jnp.log(total),0.0)
    qx_ref[...]=jnp.concatenate([q[:,:hi],q[:,hi:]+parts(-lse,cols,hi)],axis=1)

def const(a): return pl.BlockSpec(a.shape,lambda i,sc:(0,)*a.ndim)

def attn_fwd(scal, packed, shard, nh=3, bq=512):
    T=packed.shape[0]; W=packed.shape[1]//3
    tabs=tables(nh,W)
    def where(i,sc):
        per=shard//bq
        return (jnp.bitwise_xor(i//per,sc[0])*per+i%per,0)
    return pl.pallas_call(
        functools.partial(fwd_kernel,nh,bq,shard),
        grid_spec=pltpu.PrefetchScalarGridSpec(num_scalar_prefetch=1,grid=(T//bq,),
            in_specs=[once(packed)]+[once(a) for a in tabs],
            out_specs=[pl.BlockSpec((shard,nh*HD),lambda i,sc:(0,0))]*(T//shard)+[pl.BlockSpec((bq,W),where)],
            scratch_shapes=[pltpu.VMEM((nh,bq,W),BF),pltpu.VMEM((T,W),BF),pltpu.VMEM((nh,T,W),BF),
                pltpu.VMEM((8,LANES),F32),pltpu.VMEM((bq,LANES),F32),pltpu.VMEM((bq,W),F32)]),
        out_shape=[jax.ShapeDtypeStruct((shard,nh*HD),BF)]*(T//shard)+[jax.ShapeDtypeStruct((T,W),BF)],
        compiler_params=pltpu.CompilerParams(vmem_limit_bytes=56*2**20),
        name="attention_forward",
    )(scal,packed,*tabs)

def bwd_kernel(nh,heads,n,bk,shard,sc_ref,qx_ref,p_ref,*refs):
    o_refs=refs[:n]; g_refs=refs[n:2*n]; mask_ref,fold_ref=refs[2*n:2*n+2]
    old_ref=refs[2*n+2] if len(refs)>2*n+8 else None
    out_ref,q_s,d_s,dq_s,dk_s,dv_s=refs[-6:]; m=len(heads)
    T=p_ref.shape[0]; W=p_ref.shape[1]//3; hi=W-LANES; cols=nh*HD
    j=pl.program_id(0)
    @pl.when(j==0)
    def _():
        for c in range(0,T,512):
            qx=qx_ref[c:c+512,:]
            g=g_refs[c//shard][c%shard:c%shard+512,:]
            og=o_refs[c//shard][c%shard:c%shard+512,:].astype(F32)*g.astype(F32)
            og1=og.astype(BF); og2=(og-og1.astype(F32)).astype(BF)
            delta=dot(og1,fold_ref[:cols,:],NN)+dot(og2,fold_ref[:cols,:],NN)
            gx=jnp.concatenate([g,jnp.zeros((512,W-cols),BF)],axis=1)
            gx=jnp.concatenate([gx[:,:hi],gx[:,hi:]+parts(-delta,cols,hi)],axis=1)
            for i,h in enumerate(heads):
                q_s[i,c:c+512,:]=qx*mask_ref[h:h+1,:]
                d_s[i,c:c+512,:]=gx*mask_ref[h:h+1,:]
            dq_s[:,c:c+512]=jnp.zeros((m*HD,512),F32)
    start=j*bk
    row_start,valid_end,row_end=row_info(sc_ref,start)
    at=place(sc_ref,start,shard)
    k0=p_ref[pl.ds(at,bk),W:2*W]
    k=k0+mask_ref[nh:nh+1,:]; v=p_ref[pl.ds(at,bk),2*W:]+mask_ref[nh:nh+1,:]
    kt=jnp.transpose(k0)
    def step(i,kind):
        b=start+i*bk
        bt=place(sc_ref,b,shard)
        if kind!=0:
            krow=lax.broadcasted_iota(jnp.int32,(bk,bk),0); qcol=lax.broadcasted_iota(jnp.int32,(bk,bk),1)
            ok=krow<valid_end-start
            if kind==2: ok=(krow==qcol)|((krow<qcol)&ok)
        ps=[];dss=[]
        for i,h in enumerate(heads):
            s=dot(k,q_s[i,pl.ds(bt,bk),:],NT)
            if kind!=0: s=jnp.where(ok,s,-1e30)
            p=jnp.exp(s)
            ds=(p*dot(v,d_s[i,pl.ds(bt,bk),:],NT)).astype(BF)
            ps.append(p.astype(BF)); dss.append(ds)
            dq_s[i*HD:(i+1)*HD,pl.ds(bt,bk)]+=dot(kt[h*HD:(h+1)*HD],ds,NN)
        dv=dot(jnp.concatenate(ps,axis=1),d_s[:,pl.ds(bt,bk),:].reshape(m*bk,W),NN)
        dk=dot(jnp.concatenate(dss,axis=1),q_s[:,pl.ds(bt,bk),:].reshape(m*bk,W),NN)
        if kind==2: dv_s[...]=dv; dk_s[...]=dk
        else: dv_s[...]+=dv; dk_s[...]+=dk
    after=(row_end-start)//bk
    n_off=jnp.where(valid_end>start,after,1)
    step(0,2)
    whole=valid_end>=start+bk
    lax.fori_loop(1,jnp.where(whole,after,1),lambda i,c:(step(i,0),c)[1],0)
    lax.fori_loop(1,jnp.where(whole,1,n_off),lambda i,c:(step(i,1),c)[1],0)
    keep=(lax.broadcasted_iota(jnp.int32,(bk,W),1)<cols)
    def put(rows,at_lane,x):
        x=x.astype(BF)
        if old_ref is not None: x=x+old_ref[rows,at_lane:at_lane+W]
        out_ref[rows,at_lane:at_lane+W]=x
    put(pl.ds(at,bk),W,jnp.where(keep,dk_s[...],0.0))
    put(pl.ds(at,bk),2*W,jnp.where(keep,dv_s[...],0.0))
    @pl.when(j==pl.num_programs(0)-1)
    def _():
        for c in range(0,T,512):
            first=heads[0]*HD; rest=W-first-m*HD
            x=dq_s[:,c:c+512]
            if first: x=jnp.concatenate([jnp.zeros((first,512),F32),x],axis=0)
            if rest: x=jnp.concatenate([x,jnp.zeros((rest,512),F32)],axis=0)
            put(slice(c,c+512),0,jnp.transpose(x))

def once(a): return pl.BlockSpec(a.shape,lambda i,sc:(0,)*a.ndim,pipeline_mode=pl.Buffered(1))

def attn_bwd(scal,qx,packed,attn,grads,shard,nh,heads,old=None,bk=512):
    T=packed.shape[0]; W=packed.shape[1]//3; m=len(heads)
    masks,fold,spread=tables(nh,W)
    more=[] if old is None else [old]
    args=[qx,packed,*attn,*grads,masks,fold]+more
    return pl.pallas_call(
        functools.partial(bwd_kernel,nh,heads,len(grads),bk,shard),
        grid_spec=pltpu.PrefetchScalarGridSpec(num_scalar_prefetch=1,grid=(T//bk,),
            in_specs=[once(x) for x in args],
            out_specs=const(packed),
            scratch_shapes=[pltpu.VMEM((m,T,W),BF),pltpu.VMEM((m,T,W),BF),pltpu.VMEM((m*HD,T),F32),
                pltpu.VMEM((bk,W),F32),pltpu.VMEM((bk,W),F32)]),
        out_shape=jax.ShapeDtypeStruct(packed.shape,BF),
        compiler_params=pltpu.CompilerParams(vmem_limit_bytes=60*2**20),
        name="attention_backward",
    )(scal,*args)


EPSILON = 1e-05
TN=(((0,),(0,)),((),()))
VMEM_LIMIT=60*2**20


def widen(ref, buf):
    buf[:,:ref.shape[1]]=ref[...].astype(F32)
    lane=lax.broadcasted_iota(jnp.int32,buf.shape,1)
    return jnp.where(lane<ref.shape[1],buf[...],0.0)

def closed(x):
    lane=lax.broadcasted_iota(jnp.int32,x.shape,1)
    return jnp.where(lane<x.shape[1]-1,x,-jnp.sum(x,axis=1,keepdims=True))

def last_off(x):
    return x-x[:,x.shape[1]-1:]

def centred(x):
    return x-jnp.mean(x,axis=1,keepdims=True)

def inverse(z):
    return lax.rsqrt(jnp.mean(z*z,axis=1,keepdims=True)+EPSILON)

def norm_pull(grad,hat,inv,gain):
    dh=grad*gain
    return last_off((dh-hat*jnp.mean(dh*hat,axis=1,keepdims=True))*inv)

def first_norm_kernel(x_ref,gain_ref,n_ref,buf):
    z=closed(widen(x_ref,buf))
    n_ref[...]=(z*inverse(z)*gain_ref[...]).astype(BF)

def first_norm(stream,gain):
    T,C=stream.shape; R=min(T,256)
    return pl.pallas_call(first_norm_kernel,grid=(T//R,),
        in_specs=[pl.BlockSpec((R,C),lambda i:(i,0)),pl.BlockSpec((1,C+1),lambda i:(0,0))],
        out_specs=pl.BlockSpec((R,C+1),lambda i:(i,0)),
        out_shape=jax.ShapeDtypeStruct((T,C+1),BF),
        scratch_shapes=[pltpu.VMEM((R,C+1),F32)],name="first_norm")(stream,gain)

def project_kernel(sc_ref,x_ref,y_ref,w_ref,*refs):
    out_ref=refs[-1]
    @pl.when(pl.program_id(0)==0)
    def _(): out_ref[...]=dot(x_ref[...],w_ref[...],NN).astype(BF)
    @pl.when(pl.program_id(0)==1)
    def _(): out_ref[...]=dot(y_ref[...],w_ref[...],NN).astype(BF)

def project(scal,x,y,w,count,at,old=None):
    T,D=x.shape; N=w.shape[1]
    more=[] if old is None else [old]
    return pl.pallas_call(project_kernel,
        grid_spec=pltpu.PrefetchScalarGridSpec(num_scalar_prefetch=1,grid=(2,),
            in_specs=[const(x),const(y),const(w)]+[pl.BlockSpec(memory_space=pl.ANY)]*len(more),
            out_specs=pl.BlockSpec((T,N),lambda i,sc:(at+i,0))),
        out_shape=jax.ShapeDtypeStruct((count*T,N),BF),
        input_output_aliases={4:0} if more else {},
        compiler_params=pltpu.CompilerParams(vmem_limit_bytes=VMEM_LIMIT),
        name="project")(scal,x,y,w,*more)

def last_norm_kernel(x_ref,mid_ref,a_ref,b_ref,c_ref,gain_ref,out_ref,buf):
    z=closed(widen(x_ref,buf))
    inv=inverse(z)
    grad=(a_ref[...].astype(F32)+b_ref[...].astype(F32))+c_ref[...].astype(F32)
    out=mid_ref[...]+norm_pull(grad,z*inv,inv,gain_ref[...])
    out_ref[...]=out[:,:out_ref.shape[1]]

def last_norm(stream,middle,terms,gain):
    T,C=stream.shape; R=min(T,256)
    row=lambda w: pl.BlockSpec((R,w),lambda i:(i,0))
    return pl.pallas_call(last_norm_kernel,grid=(T//R,),
        in_specs=[row(C)]+[row(C+1)]*4+[pl.BlockSpec((1,C+1),lambda i:(0,0))],
        out_specs=row(C),out_shape=jax.ShapeDtypeStruct((T,C),F32),
        scratch_shapes=[pltpu.VMEM((R,C+1),F32)],name="last_norm")(stream,middle,*terms,gain)

def piece_order(n):
    return [i for i in range(n) if i&1]+[i for i in range(n) if not i&1]

def middle_kernel(n,R,sc_ref,x_ref,c_ref,gain_ref,*refs):
    attn=refs[:n]; outw=refs[n:2*n]; weights=refs[2*n:3*n]; gh=refs[3*n:4*n]
    res_ref,mid_ref,send_ref,keep_ref,go_ref,sum_ref,buf,z_s,n_s,g_s,bm_s,gn_s,w_s,wu_s,wd_s,sem=refs[4*n:]
    T,D=z_s.shape; H=attn[0].shape[1]; FD=w_s.shape[1]//2; tiles=T//R
    k=pl.program_id(0); order=piece_order(n)
    lane=lax.broadcasted_iota(jnp.int32,(R,D),1)
    def fetch(s,slot): return pltpu.make_async_copy(weights[s].at[H:,:],w_s.at[slot],sem.at[slot])
    def rows(r): return pl.ds(pl.multiple_of(r*R,R),R)
    def valid_rows(r):
        start=sc_ref[16]+r*R
        return lax.broadcasted_iota(jnp.int32,(R,D),0)<row_info(sc_ref,start)[1]-start
    def grad_out(r):
        buf[:,:D-1]=c_ref[rows(r),:].astype(F32)
        return jnp.where((lane<D-1)&valid_rows(r),buf[...],0.0)
    def squares(x,r):
        x=jnp.where(valid_rows(r),x,0.0)
        return jnp.sum((x*x).reshape(R//8,8,D),axis=0)
    @pl.when(k==0)
    def _():
        fetch(order[0],0).start()
        sum_ref[...]=jnp.zeros_like(sum_ref)
        def first(r,carry):
            at=rows(r)
            buf[:,:D-1]=x_ref[at,:].astype(F32)
            z1=closed(jnp.where(lane<D-1,buf[...],0.0))
            ba=sum(dot(attn[s][at,:],outw[s][...],NN) for s in range(n))
            z2=z1+centred(ba)
            z_s[at,:]=z2
            n_s[at,:]=(z2*inverse(z2)*gain_ref[...]).astype(BF)
            g_s[at,:]=centred(grad_out(r)).astype(BF)
            bm_s[at,:]=jnp.zeros((R,D),F32); gn_s[at,:]=jnp.zeros((R,D),F32)
            sum_ref[16:24,:]+=squares(ba,r)
            return carry
        lax.fori_loop(0,tiles,first,0)
    slot=k%2
    for s in range(n):
        @pl.when(k==s)
        def _():
            fetch(order[s],s%2).wait()
            if s+1<n: fetch(order[s+1],(s+1)%2).start()
    def piece(r,carry):
        at=rows(r)
        nr=n_s[at,:]; gr=g_s[at,:]
        up=w_s[slot,:FD,:]; down=w_s[slot,FD:,:]
        x=dot(nr,up,NN)
        sq=x*x
        th=jnp.tanh(x*(0.7978845608028654+0.035677408136300125*sq))
        half=0.5+0.5*th
        hid=(x*half).astype(BF)
        slope=half+0.5*x*(1.0-th*th)*(0.7978845608028654+0.10703222440890037*sq)
        gp=(dot(gr,down,NT)*slope).astype(BF)
        bm_s[at,:]+=dot(hid,down,NN); gn_s[at,:]+=dot(gp,up,NT)
        wu_s[...]+=dot(nr,gp,TN); wd_s[...]+=dot(hid,gr,TN)
        return carry
    wu_s[...]=jnp.zeros_like(wu_s); wd_s[...]=jnp.zeros_like(wd_s)
    lax.fori_loop(0,tiles,piece,0)
    def put(ref):
        ref[0,:FD,:]=wu_s[...].astype(BF); ref[0,FD:,:]=wd_s[...].astype(BF)
    pl.when(k<n//2)(functools.partial(put,send_ref))
    pl.when(k>=n//2)(functools.partial(put,keep_ref))
    @pl.when(k==n-1)
    def _():
        def final(r,carry):
            at=rows(r)
            z2=z_s[at,:]; inv=inverse(z2); hat=z2*inv; gn=gn_s[at,:]; bm=bm_s[at,:]
            out=z2+centred(bm)
            res_ref[at,:]=out[:,:D-1].astype(BF)
            mid=grad_out(r)+norm_pull(gn,hat,inv,gain_ref[...])
            mid_ref[at,:]=mid
            ga=centred(mid).astype(BF)
            g_s[at,:]=ga
            for s in range(n): gh[s][at,:]=dot(ga,outw[s][...],NT).astype(BF)
            sum_ref[0:8,:]+=jnp.sum((gn*hat).reshape(R//8,8,D),axis=0)
            sum_ref[8:16,:]+=squares(out,r); sum_ref[24:32,:]+=squares(bm,r)
            return carry
        lax.fori_loop(0,tiles,final,0)
        for s in range(n): go_ref[s]=dot(attn[order[s]][...],g_s[...],TN).astype(BF)

def middle_part(scal,stream,cotangent,gain,attn,weights,R=256):
    n=len(attn); T,H=attn[0].shape; D=stream.shape[1]+1; FD=(weights[0].shape[0]-H)//2; R=min(R,T)
    once=lambda a: pl.BlockSpec(a.shape,lambda i,sc:(0,)*a.ndim,pipeline_mode=pl.Buffered(1))
    whole=lambda *s: pl.BlockSpec(s,lambda i,sc:(0,)*len(s))
    top=pl.BlockSpec((H,D),lambda i,sc:(0,0),pipeline_mode=pl.Buffered(1))
    return pl.pallas_call(
        functools.partial(middle_kernel,n,R),
        grid_spec=pltpu.PrefetchScalarGridSpec(num_scalar_prefetch=1,grid=(n,),
            in_specs=[once(stream),once(cotangent),once(gain)]+[once(a) for a in attn]+[top]*n+[pl.BlockSpec(memory_space=pl.ANY)]*n,
            out_specs=[whole(T,H)]*n+[whole(T,D-1),whole(T,D),pl.BlockSpec((1,2*FD,D),lambda i,sc:(jnp.minimum(i,n//2-1),0,0)),
                pl.BlockSpec((1,2*FD,D),lambda i,sc:(jnp.maximum(i-n//2,0),0,0)),whole(n,H,D),whole(32,D)],
            scratch_shapes=[pltpu.VMEM((R,D),F32),pltpu.VMEM((T,D),F32),pltpu.VMEM((T,D),BF),pltpu.VMEM((T,D),BF),pltpu.VMEM((T,D),F32),pltpu.VMEM((T,D),F32),
                pltpu.VMEM((2,2*FD,D),BF),pltpu.VMEM((D,FD),F32),pltpu.VMEM((FD,D),F32),pltpu.SemaphoreType.DMA((2,))]),
        out_shape=[jax.ShapeDtypeStruct((T,H),BF)]*n+[jax.ShapeDtypeStruct((T,D-1),BF),jax.ShapeDtypeStruct((T,D),F32),
            jax.ShapeDtypeStruct((n//2,2*FD,D),BF),jax.ShapeDtypeStruct((n//2,2*FD,D),BF),jax.ShapeDtypeStruct((n,H,D),BF),jax.ShapeDtypeStruct((32,D),F32)],
        compiler_params=pltpu.CompilerParams(vmem_limit_bytes=VMEM_LIMIT),
        name="middle",
    )(scal,stream,cotangent,gain,*attn,*weights,*weights)


def swap(x,axis,step):
    size=lax.axis_size(axis)
    return lax.ppermute(x,axis,[(i,i^step) for i in range(size)])

def after(x,*others):
    return lax.optimization_barrier((x,)+others)[0]

def choose(options,index):
    out=options[0]
    for i in range(1,len(options)): out=jnp.where(index==i,options[i],out)
    return out

def bit_groups(size):
    bits=[1<<b for b in range(size.bit_length()-1)]
    groups=[bits[:1]]; rest=bits[1:]
    while rest: groups.append(rest[:2]); rest=rest[2:]
    return [g for g in groups if g]

def sum_over(x,axis,first):
    me=lax.axis_index(axis); levels=[]
    cur=x
    for bits in bit_groups(lax.axis_size(axis)):
        m=1<<len(bits); low=bits[0]
        mine=(me//low)%m
        rows=cur.shape[0]//m
        cut=[cur[i*rows:(i+1)*rows] for i in range(m)]
        total=choose(cut,mine)
        for d in range(1,m):
            total=total+swap(choose([cut[i^d] for i in range(m)],mine).astype(BF),axis,d*low).astype(F32)
        levels.append((m,low,mine)); cur=total
    cur,first=lax.optimization_barrier((cur.astype(BF),first))
    for m,low,mine in reversed(levels):
        got=[cur]+[swap(cur,axis,d*low) for d in range(1,m)]
        cur=jnp.concatenate([choose([got[i^p] for i in range(m)],mine) for p in range(m)],axis=0)
    return cur.astype(F32),first

def butterfly(x,axis):
    step=1
    while step<lax.axis_size(axis):
        x=x+swap(x,axis,step); step*=2
    return x

def shards(stream,cotangent,bucket,row_counts,lengths,w_qkv,w_out,w_up,w_down,gain_one,gain_two):
    T=stream.shape[0]; D=stream.shape[1]+1; C=w_qkv.shape[2]; nh=C//HD
    n=lax.axis_size("tensor"); t=lax.axis_index("tensor")
    wide=-(-(C+4*nh)//LANES)*LANES
    span=BASE*jnp.where(bucket[0]==0,1,jnp.where(bucket[0]==1,2,4)).astype(jnp.int32)
    zero=jnp.zeros((),jnp.int32)
    scal=jnp.stack([t.astype(jnp.int32),span,row_counts[0]]+[lengths[0,r] for r in range(lengths.shape[1])]+[zero]*(13-lengths.shape[1])+[(t*T).astype(jnp.int32)])
    g1=gain_one.reshape(1,D); g2=gain_two.reshape(1,D)
    lift=np.ones((1,3,1),np.float32); lift[0,0]=HD**-0.5
    w_pad=jnp.pad(w_qkv*jnp.asarray(lift,BF),((0,0),(0,0),(0,wide-C))).reshape(D,3*wide)

    normed=first_norm(stream,g1)
    far=swap(normed,"tensor",2); near=swap(normed,"tensor",1)
    own_w=after(jnp.concatenate([w_out,w_up,w_down],axis=0),far)
    far_w=swap(own_w,"tensor",2); near_w=swap(own_w,"tensor",1)
    corner=swap(far,"tensor",1)
    packed=project(scal,normed,near,w_pad,n,0)
    packed=project(scal,far,corner,w_pad,n,2,packed)
    *heads_out,qx=attn_fwd(scal,packed,T,nh)
    attn=[heads_out[0]]+[swap(heads_out[d],"tensor",d) for d in range(1,n)]
    weights=[own_w,near_w,far_w,swap(after(far_w,attn[1]),"tensor",1)]
    *grad_heads,result,mid,w_send,w_keep,go,sums=middle_part(scal,stream,cotangent,g2,attn,weights)
    heads=[grad_heads[0]]+[swap(grad_heads[d],"tensor",d) for d in range(1,n)]
    w_send,go_send=lax.optimization_barrier((w_send,go[:n//2],heads[1]))[:2]
    w_got=swap(w_send,"tensor",1); o_got=swap(go_send,"tensor",1)
    R=C+w_keep.shape[1]; q=lax.axis_size("dp"); r=R//q
    flat=lambda x: x.reshape(q,-1,D)
    w_half=(w_keep.astype(F32)+w_got.astype(F32)).astype(BF); o_half=(go[n//2:].astype(F32)+o_got.astype(F32)).astype(BF)
    w_half=jnp.concatenate([flat(x) for i in range(2) for x in (o_half[i],w_half[i,:D],w_half[i,D:])],axis=1).reshape(2*R,D)
    w_part=lax.psum_scatter(w_half,"dp",scatter_dimension=0,tiled=True)

    grad_packed=attn_bwd(scal,qx,packed,heads_out,heads,T,nh,list(range(nh)))
    back={i:dot(grad_packed[i*T:(i+1)*T],w_pad,NT).astype(BF) for i in piece_order(n)}
    near_b={i:swap(back[i^1],"tensor",1) for i in (0,2)}
    two=(back[2].astype(F32)+near_b[2].astype(F32)).astype(BF)
    far_b=swap(two,"tensor",2)
    gathered=jnp.concatenate([normed,near,far,corner],axis=0)
    gq=dot(gathered,after(grad_packed,two),TN)
    gq=gq.reshape(D,3,wide)[:,:,:C]*lift
    gain_part=jnp.sum(gq*w_qkv.astype(F32),axis=(1,2))/gain_one
    w_other=swap(w_part[r:],"tensor",2)
    w_own=(w_part[:r].astype(F32)+w_other.astype(F32)).astype(BF)
    w_sum=lax.all_gather(w_own,"dp",axis=0).astype(F32)
    grad_stream=last_norm(stream,mid,[back[0],near_b[0],far_b],g1)
    gq,grad_stream=sum_over(gq.reshape(D,3*C),"dp",grad_stream)
    gq=gq.reshape(D,3,C)
    cut=[0]
    for part in (C,D,w_keep.shape[1]-D): cut.append(cut[-1]+part//q)
    g_out,g_up,g_down=[w_sum[:,i:j].reshape(-1,D) for i,j in zip(cut[:-1],cut[1:])]
    group_tokens=jnp.sum(jnp.where(jnp.arange(lengths.shape[1])<row_counts[0],lengths[0],0)).astype(F32)/n
    s=sums.reshape(4,8,D)
    small=jnp.concatenate([gain_part,jnp.sum(s[0],axis=0),jnp.sum(s[1:],axis=(1,2)),group_tokens[None]])
    small=jnp.pad(small,(0,-small.shape[0]%LANES)).reshape(-1,LANES)
    small=butterfly(butterfly(small,"tensor"),"dp").reshape(-1)
    root=jnp.sqrt(small[2*D:2*D+3]/(D*small[2*D+3]))
    return (result,grad_stream,gq,g_out,g_up,g_down,small[:D],small[D:2*D],root)


def solution(mesh):
    rows=P(("dp","tensor"),None)
    return jax.shard_map(shards,mesh=mesh,
        in_specs=(rows,rows,P("dp"),P("dp"),P("dp",None),P(None,None,"tensor"),P("tensor",None),P(None,"tensor"),P("tensor",None),P(),P()),
        out_specs=(rows,rows,P(None,None,"tensor"),P("tensor",None),P(None,"tensor"),P("tensor",None),P(),P(),P()),
        check_vma=False)
```

time: 802 us -> 503 us (0.63)
  starting transfers between devices: 179 us -> 39 us
  waiting for transfers between devices: 193 us -> 131 us
  Pallas kernels: 294 us -> 239 us
  local copies, waits for them, and re-layouts: 56.5 us -> 30.2 us
  other arithmetic: 31.2 us -> 14 us
    ppermute x31, starting transfers between devices: 179 us -> 38.9 us  [swap(): return lax.ppermute(x, axis, [(i, i ^ step) for i in range(size)])]
    pallas_call x3 -> x5, Pallas kernels: 262 us -> 179 us  [the longest x1 103 us: attn_bwd(): pl.pallas_call(functools.partial(bwd_kernel, nh, heads, len(grads), bk, s...]
    ppermute x31, waiting for transfers between devices: 166 us -> 131 us  [swap(): return lax.ppermute(x, axis, [(i, i ^ step) for i in range(size)])]
    pallas_call x1, Pallas kernels: 28.1 us -> 56.7 us  [attn_fwd(): pl.pallas_call(functools.partial(fwd_kernel, nh, bq, shard), grid_spec=pl...]
    psum x1 -> x0, waiting for transfers between devices: 26.4 us -> none  [shards(): gw_sum = lax.psum(gw_own, 'dp').astype(F32)]
    dynamic_update_slice x5 -> x0, local copies, waits for them, and re-layouts: 22.7 us -> none  [the longest x4 11.4 us: sum_over(): lax.dynamic_update_index_in_dim(full, swap(cur, axis, d * low), mine ^ d, 0)]
    dot_general x3 -> x5, matrix products: 27.3 us -> 26 us  [dot(): return lax.dot_general(a, b, dims, preferred_element_type=F32)]
  transfers between devices with their start and end apart: 32 -> 33, of which waited for: 14 -> 17; matrix products, arithmetic and copies ran while one was open for 12% -> 10% of each run, Pallas kernels for 10% -> 36%
where the time goes in v2:
time: 503 us; the launch traced here: 497 us
  Pallas kernels  239 us (48%)
  waiting for transfers between devices  131 us (26%)
  starting transfers between devices  39 us (8%)
  local copies, waits for them, and re-layouts  30.2 us (6%)
  matrix products  26 us (5%)
  between operations  17.3 us (3%)
  other arithmetic  14 us (3%)
    ppermute x31, waiting for transfers between devices, swap(): return lax.ppermute(x, axis, [(i, i ^ step) for i in range(size)])  131 us
    pallas_call x1, Pallas kernels, attn_bwd(): pl.pallas_call(functools.partial(bwd_kernel, nh, heads, len(grads), bk, s...  103 us
    pallas_call x1, Pallas kernels, attn_fwd(): pl.pallas_call(functools.partial(fwd_kernel, nh, bq, shard), grid_spec=pl...  56.7 us
    pallas_call x1, Pallas kernels, middle_part(): pl.pallas_call(functools.partial(middle_kernel, n, R), grid_spec=pltpu.Pr...  55.3 us
    ppermute x31, starting transfers between devices, swap(): return lax.ppermute(x, axis, [(i, i ^ step) for i in range(size)])  38.9 us
    dot_general x5, matrix products, dot(): return lax.dot_general(a, b, dims, preferred_element_type=F32)  26 us
    pallas_call x2, Pallas kernels, project(): pl.pallas_call(project_kernel, grid_spec=pltpu.PrefetchScalarGridSpec(num...  13.7 us
  transfers between devices with their start and end apart: 33, of which 17 were waited for; matrix products, arithmetic and copies ran while one was open for 10% of the time, Pallas kernels for 36%

profile of v2, /device:TPU:0, one launch (start us, length us, event | category | flops | bytes accessed | tf_op | source)
XLA Modules:
  0.0 496.5 jit_solution(9617260664223483481)
XLA Ops:
  7.2 1.3 reshape.81.gain_ref
  8.5 4.0 first_norm.1.x_ref
  12.5 2.9 collective-permute-start
  15.5 1.8 pad_maximum_fusion.refs_4_.refs_8_
  17.3 32.8 %collective-permute-done.x_ref = bf16[1024,768]{1,0:T(8,128)(2,1)} collective-permute-done((bf16[1024,768]{1,0:T(8,128)(2,1)}, bf16[1024,768]{1,0:T(8,128)(2,1)}, u32[]{:S(2)}, u32[]{:S(2)}) %collective-permute-start) | collective-permute-done | bytes 1572896 | tf_op jit(solution)/shard_map/ppermute | solution.py:410
  50.2 1.7 collective-permute-start.7
  53.9 1.1 pad.8
  55.0 2.4 copy.30.w_ref
  58.0 3.2 stack.12.sc_ref
  61.2 6.9 %project.2.refs_0_ = bf16[4096,768]{1,0:T(8,128)(2,1)} custom-call(s32[17]{0:T(128)} %stack.12.sc_ref, bf16[1024,768]{1,0:T(8,128)(2,1)} %first_norm.1.x_ref, bf16[1024,768]{1,0:T(8,128)(2,1)} %collective-permute-done.2.y_ref, bf16[768,768]{1,0:T(8,128)(2,1)} %copy.30.w_ref), custom_call_target="tpu_custom_call" | custom-call | tf_op jit(solution)/shard_map/project/pallas_call | solution.py:283
  68.1 6.9 %project.3.p_ref = bf16[4096,768]{1,0:T(8,128)(2,1)} custom-call(s32[17]{0:T(128)} %stack.12.sc_ref, bf16[1024,768]{1,0:T(8,128)(2,1)} %collective-permute-done.x_ref, bf16[1024,768]{1,0:T(8,128)(2,1)} %collective-permute-done.1.y_ref, bf16[768,768]{1,0:T(8,128)(2,1)} %copy.30.w_ref, bf16[4096,768]{1,0:T(8,128)(2,1)} %project.2.refs_0_), custom_call_target="tpu_custom_call", output_to_operand_aliasing={{}: (4, {})} | custom-call | tf_op jit(solution)/shard_map/project/pallas_call | solution.py:283
  74.9 56.7 %attention_forward.1 = (bf16[1024,192]{1,0:T(8,128)(2,1)}, bf16[1024,192]{1,0:T(8,128)(2,1)}, bf16[1024,192]{1,0:T(8,128)(2,1)}, bf16[1024,192]{1,0:T(8,128)(2,1)}, bf16[4096,256]{1,0:T(8,128)(2,1)}) custom-call(s32[17]{0:T(128)} %stack.12.sc_ref, bf16[4096,768]{1,0:T(8,128)(2,1)} %project.3.p_ref, bf16[8,256]{1,0:T(8,128)(2,1)} %constant.91.clone.mask_ref.refs_8_, ...), custom_call_target="tpu_custom_call" | custom-call | tf_op jit(solution)/shard_map/attention_forward/pallas_call | solution.py:135
  132.1 1.6 collective-permute-done.3.refs_1_
  134.2 1.4 collective-permute-start.5
  136.2 12.7 %collective-permute-done.4.refs_2_ = bf16[1024,192]{1,0:T(8,128)(2,1)S(1)} collective-permute-done((bf16[1024,192]{1,0:T(8,128)(2,1)}, bf16[1024,192]{1,0:T(8,128)(2,1)S(1)}, u32[]{:S(2)}, u32[]{:S(2)}) %collective-permute-start.4) | collective-permute-done | bytes 393248 | tf_op jit(solution)/shard_map/ppermute | solution.py:410
  148.8 10.1 %collective-permute-done.5.refs_3_ = bf16[1024,192]{1,0:T(8,128)(2,1)S(1)} collective-permute-done((bf16[1024,192]{1,0:T(8,128)(2,1)}, bf16[1024,192]{1,0:T(8,128)(2,1)S(1)}, u32[]{:S(2)}, u32[]{:S(2)}) %collective-permute-start.5) | collective-permute-done | bytes 393248 | tf_op jit(solution)/shard_map/ppermute | solution.py:410
  158.9 1.6 copy-done.1
  160.7 1.5 copy-done.2
  162.1 55.3 %middle.1 = (bf16[1024,192]{1,0:T(8,128)(2,1)}, bf16[1024,192]{1,0:T(8,128)(2,1)}, bf16[1024,192]{1,0:T(8,128)(2,1)}, bf16[1024,192]{1,0:T(8,128)(2,1)}, bf16[10...) custom-call(s32[17]{0:T(128)} %stack.12.sc_ref, ...), custom_call_target="tpu_custom_call" | custom-call | tf_op jit(solution)/shard_map/middle/pallas_call | solution.py:393
  217.9 1.3 slice.128
  220.2 6.1 %collective-permute-done.23 = bf16[2,192,768]{2,1,0:T(8,128)(2,1)S(1)} collective-permute-done((bf16[2,192,768]{2,1,0:T(8,128)(2,1)S(1)}, bf16[2,192,768]{2,1,0:T(8,128)(2,1)S(1)}, u32[]{:S(2)}, u32[]{:S(2)}) %collective-permute-start.23) | collective-permute-done | bytes 589856 | tf_op jit(solution)/shard_map/ppermute | solution.py:410
  226.3 1.2 add_convert_fusion.2
  227.5 0.8 constant_dynamic-update-slice_fusion.5
  228.6 1.4 add_convert_fusion
  230.4 1.1 constant_dynamic-update-slice_fusion.4
  231.5 1.1 constant_dynamic-update-slice_fusion.3
  233.4 1.1 constant_dynamic-update-slice_fusion.1
  234.4 1.1 constant_dynamic-update-slice_fusion
  235.7 1.0 copy-done.21
  236.9 1.4 collective-permute-start.11
  238.4 13.0 %collective-permute-done.10.refs_6_ = bf16[1024,192]{1,0:T(8,128)(2,1)S(1)} collective-permute-done((bf16[1024,192]{1,0:T(8,128)(2,1)S(1)}, bf16[1024,192]{1,0:T(8,128)(2,1)S(1)}, u32[]{:S(2)}, u32[]{:S(2)}) %collective-permute-start.10) | collective-permute-done | bytes 393248 | tf_op jit(solution)/shard_map/ppermute | solution.py:410
  251.4 10.1 %collective-permute-done.11.refs_7_ = bf16[1024,192]{1,0:T(8,128)(2,1)S(1)} collective-permute-done((bf16[1024,192]{1,0:T(8,128)(2,1)S(1)}, bf16[1024,192]{1,0:T(8,128)(2,1)S(1)}, u32[]{:S(2)}, u32[]{:S(2)}) %collective-permute-start.11) | collective-permute-done | bytes 393248 | tf_op jit(solution)/shard_map/ppermute | solution.py:410
  261.5 0.8 copy-done.13
  262.3 102.5 %attention_backward.1 = bf16[4096,768]{1,0:T(8,128)(2,1)} custom-call(s32[17]{0:T(128)} %stack.12.sc_ref, bf16[4096,256]{1,0:T(8,128)(2,1)} %get-tuple-element.38.qx_ref, bf16[4096,768]{1,0:T(8,128)(2,1)} %project.3.p_ref, bf16[1024,192]{1,0:T(8,128)(2,1)} %get-tuple-element.31.refs_0_, bf16[1024,192]{1,0:T(8,128)(2,1)} %get-tuple-element.32.refs_1_, ...), custom_call_target="tpu_custom_call" | custom-call | tf_op jit(solution)/shard_map/attention_backward/pallas_call | solution.py:221
  364.8 4.0 convolution_convert_fusion.2
  368.8 0.8 collective-permute-start.12
  371.3 3.9 convolution_convert_fusion
  375.2 3.9 convolution_convert_fusion.3
  379.2 1.0 slice.166
  380.6 2.9 add_convert_fusion.1
  383.5 1.7 collective-permute-start.18
  385.2 5.6 %collective-permute-done.25 = bf16[216,768]{1,0:T(8,128)(2,1)S(1)} collective-permute-done((bf16[216,768]{1,0:T(8,128)(2,1)S(1)}, bf16[216,768]{1,0:T(8,128)(2,1)S(1)}, u32[]{:S(2)}, u32[]{:S(2)}) %collective-permute-start.25) | collective-permute-done | bytes 331808 | tf_op jit(solution)/shard_map/ppermute | solution.py:410
  390.8 0.8 add_convert_fusion.3
  391.7 10.2 %fusion = f32[768,768]{0,1:T(8,128)S(1)} fusion(bf16[4096,768]{1,0:T(8,128)(2,1)} %attention_backward.1, bf16[1024,768]{1,0:T(8,128)(2,1)} %collective-permute-done.1.y_ref, bf16[1024,768]{1,0:T(8,128)(2,1)} %collective-permute-done.x_ref, bf16[1024,768]{1,0:T(8,128)(2,1)} %collective-permute-done.2.y_ref, bf16[1024,768]{1,0:T(8,128)(2,1)} %first_norm.1.x_ref), kind=kOutput, calls=%fused_computation.1 | convolution fusion | flops 4857004032 | bytes 14942208 | tf_op jit(solution)/shard_map/dot_general | solution.py:13
  402.6 3.9 convolution_convert_fusion.1.a_ref
  406.7 8.3 %collective-permute-done.13 = bf16[384,576]{0,1:T(8,128)(2,1)} collective-permute-done((bf16[384,576]{0,1:T(8,128)(2,1)S(1)}, bf16[384,576]{0,1:T(8,128)(2,1)}, u32[]{:S(2)}, u32[]{:S(2)}) %collective-permute-start.13) | collective-permute-done | bytes 442400 | tf_op jit(solution)/shard_map/ppermute | solution.py:410
  415.0 1.1 bitcast_add_fusion
  416.4 3.9 collective-permute-start.15
  420.8 5.1 %collective-permute-done.14 = bf16[96,576]{0,1:T(8,128)(2,1)S(1)} collective-permute-done((bf16[96,576]{0,1:T(8,128)(2,1)S(1)}, bf16[96,576]{0,1:T(8,128)(2,1)S(1)}, u32[]{:S(2)}, u32[]{:S(2)}) %collective-permute-start.14) | collective-permute-done | bytes 110624 | tf_op jit(solution)/shard_map/ppermute | solution.py:410
  426.0 2.4 collective-permute-start.27
  428.3 10.0 %collective-permute-done.15 = bf16[96,576]{0,1:T(8,128)(2,1)S(1)} collective-permute-done((bf16[96,576]{0,1:T(8,128)(2,1)S(1)}, bf16[96,576]{0,1:T(8,128)(2,1)S(1)}, u32[]{:S(2)}, u32[]{:S(2)}) %collective-permute-start.15) | collective-permute-done | bytes 110624 | tf_op jit(solution)/shard_map/ppermute | solution.py:410
  438.7 7.0 %last_norm.1 = f32[1024,767]{1,0:T(8,128)} custom-call(bf16[1024,767]{1,0:T(8,128)(2,1)} %x_ref.5, f32[1024,768]{1,0:T(8,128)} %get-tuple-element.44.mid_ref, bf16[1024,768]{1,0:T(8,128)(2,1)} %convolution_convert_fusion.1.a_ref, bf16[1024,768]{1,0:T(8,128)(2,1)} %collective-permute-done.17.b_ref, bf16[1024,768]{1,0:T(8,128)(2,1)} %collective-permute-done.18.c_ref, ...), custom_call_target="tpu_custom_call" | custom-call | tf_op jit(solution)/shard_map/last_norm/pallas_call | solution.py:302
  445.7 4.3 collective-permute-start.19
  450.0 8.8 %collective-permute-start.20 = (bf16[96,576]{0,1:T(8,128)(2,1)S(1)}, bf16[96,576]{0,1:T(8,128)(2,1)S(1)}, u32[]{:S(2)}, u32[]{:S(2)}) collective-permute-start(bf16[96,576]{0,1:T(8,128)(2,1)S(1)} %add_convert_fusion.4), channel_id=1, source_target_pairs={{0,16},{4,20},{8,24},{12,28},{16,0},{20,4},{24,8},{28,12},{1,17},{... | collective-permute-start | bytes 331784 | tf_op jit(solution)/shard_map/ppermute | solution.py:410
  459.6 3.5 collective-permute-done.28
  463.1 1.5 collective-permute-start.29
  464.6 2.5 collective-permute-done.29
  467.0 2.6 collective-permute-start.30
  469.7 1.9 collective-permute-done.30
  473.2 0.8 collective-permute-start.22
  475.1 6.5 %collective-permute-done.22 = bf16[384,576]{0,1:T(8,128)(2,1)S(1)} collective-permute-done((bf16[384,576]{0,1:T(8,128)(2,1)S(1)}, bf16[384,576]{0,1:T(8,128)(2,1)S(1)}, u32[]{:S(2)}, u32[]{:S(2)}) %collective-permute-start.22) | collective-permute-done | bytes 442400 | tf_op jit(solution)/shard_map/ppermute | solution.py:410
  482.0 1.3 maximum_convert_fusion
  483.3 4.3 fusion.17
  487.6 1.8 slice.167
  (111 shorter events, 12.8 us)
Async XLA Ops:
  7.2 372.0 %reduce-scatter.2.cloned.1.call-start = ((), (), s32[]{:S(2)}) async-start(), calls=%async_computation.1 | async-start | bytes 5971968 | tf_op jit(solution)/shard_map/reduce_scatter | solution.py:479
  12.5 41.2 %copy-start.5 = (bf16[768,3,192]{0,2,1:T(8,128)(2,1)S(1)}, bf16[768,3,192]{0,2,1:T(8,128)(2,1)}, u32[]{:S(2)}) copy-start(bf16[768,3,192]{0,2,1:T(8,128)(2,1)} %param.23) | copy-start | bytes 2654212
  12.5 41.2 %copy-start.18 = (bf16[3]{0:T(256)(128)(2,1)S(1)}, bf16[3]{0:T(256)(128)(2,1)}, u32[]{:S(2)}) copy-start(bf16[3]{0:T(256)(128)(2,1)} %constant.102) | copy-start | bytes 22
  12.5 37.6 %collective-permute-start = (bf16[1024,768]{1,0:T(8,128)(2,1)}, bf16[1024,768]{1,0:T(8,128)(2,1)}, u32[]{:S(2)}, u32[]{:S(2)}) collective-permute-start(bf16[1024,768]{1,0:T(8,128)(2,1)} %first_norm.1.x_ref), channel_id=1, source_target_pairs={{0,2},{1,3},{2,0},{3,1},{4,6},{5,7},{6,4},{7,5},{8,10},{9,11},{10,... | collective-permute-start | bytes 4718600 | tf_op jit(solution)/shard_map/ppermute | solution.py:410
  17.3 114.3 %copy-start = (bf16[1728,768]{1,0:T(8,128)(2,1)}, bf16[1728,768]{1,0:T(8,128)(2,1)S(1)}, u32[]{:S(2)}) copy-start(bf16[1728,768]{1,0:T(8,128)(2,1)S(1)} %pad_maximum_fusion.refs_4_.refs_8_) | copy-start | bytes 7962628
  50.2 83.5 %collective-permute-start.7 = (bf16[1728,768]{1,0:T(8,128)(2,1)S(1)}, bf16[1728,768]{1,0:T(8,128)(2,1)}, u32[]{:S(2)}, u32[]{:S(2)}) collective-permute-start(bf16[1728,768]{1,0:T(8,128)(2,1)S(1)} %pad_maximum_fusion.refs_4_.refs_8_), channel_id=1, source_target_pairs={{0,2},{1,3},{2,0},{3,1},{4,6},{5,7},{6,4},{7,5},{8,10},{9,11},{10,... | collective-permute-start | bytes 7962632 | tf_op jit(solution)/shard_map/ppermute | solution.py:410
  51.9 9.3 %collective-permute-start.2 = (bf16[1024,768]{1,0:T(8,128)(2,1)}, bf16[1024,768]{1,0:T(8,128)(2,1)}, u32[]{:S(2)}, u32[]{:S(2)}) collective-permute-start(bf16[1024,768]{1,0:T(8,128)(2,1)} %first_norm.1.x_ref), channel_id=1, source_target_pairs={{0,1},{1,0},{2,3},{3,2},{4,5},{5,4},{6,7},{7,6},{8,9},{9,8},{10,11... | collective-permute-start | bytes 4718600 | tf_op jit(solution)/shard_map/ppermute | solution.py:410
  51.9 16.1 %collective-permute-start.1 = (bf16[1024,768]{1,0:T(8,128)(2,1)}, bf16[1024,768]{1,0:T(8,128)(2,1)}, u32[]{:S(2)}, u32[]{:S(2)}) collective-permute-start(bf16[1024,768]{1,0:T(8,128)(2,1)} %collective-permute-done.x_ref), channel_id=1, source_target_pairs={{0,1},{1,0},{2,3},{3,2},{4,5},{5,4},{6,7},{7,6},{8,9},{9,8},{10,11... | collective-permute-start | bytes 4718600 | tf_op jit(solution)/shard_map/ppermute | solution.py:410
  53.9 3.5 copy-start.16
  74.9 60.7 %copy-start.17 = (f32[768]{0:T(1024)S(1)}, f32[768]{0:T(1024)}, u32[]{:S(2)}) copy-start(f32[768]{0:T(1024)} %param.28) | copy-start | bytes 9220
  131.6 2.1 collective-permute-start.3
  131.6 27.3 %collective-permute-start.6 = (bf16[1728,768]{1,0:T(8,128)(2,1)S(1)}, bf16[1728,768]{1,0:T(8,128)(2,1)S(1)}, u32[]{:S(2)}, u32[]{:S(2)}) collective-permute-start(bf16[1728,768]{1,0:T(8,128)(2,1)S(1)} %pad_maximum_fusion.refs_4_.refs_8_), channel_id=1, source_target_pairs={{0,1},{1,0},{2,3},{3,2},{4,5},{5,4},{6,7},{7,6},{8,9},{9,8},{10,11... | collective-permute-start | bytes 7962632 | tf_op jit(solution)/shard_map/ppermute | solution.py:410
  133.7 28.4 %copy-start.9 = (bf16[1024,192]{1,0:T(8,128)(2,1)}, bf16[1024,192]{1,0:T(8,128)(2,1)S(1)}, u32[]{:S(2)}) copy-start(bf16[1024,192]{1,0:T(8,128)(2,1)S(1)} %collective-permute-done.3.refs_1_) | copy-start | bytes 1179652
  133.7 26.8 %collective-permute-start.8 = (bf16[1728,768]{1,0:T(8,128)(2,1)}, bf16[1728,768]{1,0:T(8,128)(2,1)S(1)}, u32[]{:S(2)}, u32[]{:S(2)}) collective-permute-start(bf16[1728,768]{1,0:T(8,128)(2,1)} %collective-permute-done.7.refs_6_.refs_10_), channel_id=1, source_target_pairs={{0,1},{1,0},{2,3},{3,2},{4,5},{5,4},{6,7},{7,6},{8,9},{9,8},{10,11... | collective-permute-start | bytes 7962632 | tf_op jit(solution)/shard_map/ppermute | solution.py:410
  133.9 15.0 %collective-permute-start.4 = (bf16[1024,192]{1,0:T(8,128)(2,1)}, bf16[1024,192]{1,0:T(8,128)(2,1)S(1)}, u32[]{:S(2)}, u32[]{:S(2)}) collective-permute-start(bf16[1024,192]{1,0:T(8,128)(2,1)} %get-tuple-element.33.refs_2_), channel_id=1, source_target_pairs={{0,2},{1,3},{2,0},{3,1},{4,6},{5,7},{6,4},{7,5},{8,10},{9,11},{10,... | collective-permute-start | bytes 1179656 | tf_op jit(solution)/shard_map/ppermute | solution.py:410
  134.2 24.8 %collective-permute-start.5 = (bf16[1024,192]{1,0:T(8,128)(2,1)}, bf16[1024,192]{1,0:T(8,128)(2,1)S(1)}, u32[]{:S(2)}, u32[]{:S(2)}) collective-permute-start(bf16[1024,192]{1,0:T(8,128)(2,1)} %get-tuple-element.34.refs_3_), channel_id=1, source_target_pairs={{0,3},{1,2},{2,1},{3,0},{4,7},{5,6},{6,5},{7,4},{8,11},{9,10},{10,... | collective-permute-start | bytes 1179656 | tf_op jit(solution)/shard_map/ppermute | solution.py:410
  148.8 13.3 %copy-start.10 = (bf16[1024,192]{1,0:T(8,128)(2,1)}, bf16[1024,192]{1,0:T(8,128)(2,1)S(1)}, u32[]{:S(2)}) copy-start(bf16[1024,192]{1,0:T(8,128)(2,1)S(1)} %collective-permute-done.4.refs_2_) | copy-start | bytes 1179652
  158.9 1.7 copy-start.11
  158.9 1.6 copy-start.1
  160.6 1.5 copy-start.2
  217.5 2.2 collective-permute-start.9
  217.9 10.7 %copy-start.3 = (bf16[2,1536,768]{2,1,0:T(8,128)(2,1)S(1)}, bf16[2,1536,768]{2,1,0:T(8,128)(2,1)}, u32[]{:S(2)}) copy-start(bf16[2,1536,768]{2,1,0:T(8,128)(2,1)} %get-tuple-element.50) | copy-start | bytes 14155780
  219.7 10.4 %copy-start.8 = (bf16[1024,192]{1,0:T(8,128)(2,1)}, bf16[1024,192]{1,0:T(8,128)(2,1)S(1)}, u32[]{:S(2)}) copy-start(bf16[1024,192]{1,0:T(8,128)(2,1)S(1)} %collective-permute-done.9.refs_5_) | copy-start | bytes 1179652
  219.7 9.0 %collective-permute-start.24 = (bf16[2,1536,768]{2,1,0:T(8,128)(2,1)}, bf16[2,1536,768]{2,1,0:T(8,128)(2,1)S(1)}, u32[]{:S(2)}, u32[]{:S(2)}) collective-permute-start(bf16[2,1536,768]{2,1,0:T(8,128)(2,1)} %get-tuple-element.51), channel_id=1, source_target_pairs={{0,1},{1,0},{2,3},{3,2},{4,5},{5,4},{6,7},{7,6},{8,9},{9,8},{10,11... | collective-permute-start | bytes 14155784 | tf_op jit(solution)/shard_map/ppermute | solution.py:410
  220.1 6.2 %collective-permute-start.23 = (bf16[2,192,768]{2,1,0:T(8,128)(2,1)S(1)}, bf16[2,192,768]{2,1,0:T(8,128)(2,1)S(1)}, u32[]{:S(2)}, u32[]{:S(2)}) collective-permute-start(bf16[2,192,768]{2,1,0:T(8,128)(2,1)S(1)} %slice.128), channel_id=1, source_target_pairs={{0,1},{1,0},{2,3},{3,2},{4,5},{5,4},{6,7},{7,6},{8,9},{9,8},{10,11... | collective-permute-start | bytes 1769480 | tf_op jit(solution)/shard_map/ppermute | solution.py:410
  235.6 1.0 copy-start.21
  235.6 1.3 copy-start.20
  235.6 247.7 %all-gather.3.cloned.1.call-start = ((), (), s32[]{:S(2)}) async-start(), calls=%async_computation.2 | async-start | bytes 2985984 | tf_op jit(solution)/shard_map/all_gather | solution.py:492
  236.6 14.8 %collective-permute-start.10 = (bf16[1024,192]{1,0:T(8,128)(2,1)S(1)}, bf16[1024,192]{1,0:T(8,128)(2,1)S(1)}, u32[]{:S(2)}, u32[]{:S(2)}) collective-permute-start(bf16[1024,192]{1,0:T(8,128)(2,1)S(1)} %copy-done.21), channel_id=1, source_target_pairs={{0,2},{1,3},{2,0},{3,1},{4,6},{5,7},{6,4},{7,5},{8,10},{9,11},{10,... | collective-permute-start | bytes 1179656 | tf_op jit(solution)/shard_map/ppermute | solution.py:410
  236.9 24.6 %collective-permute-start.11 = (bf16[1024,192]{1,0:T(8,128)(2,1)S(1)}, bf16[1024,192]{1,0:T(8,128)(2,1)S(1)}, u32[]{:S(2)}, u32[]{:S(2)}) collective-permute-start(bf16[1024,192]{1,0:T(8,128)(2,1)S(1)} %copy-done.20), channel_id=1, source_target_pairs={{0,3},{1,2},{2,1},{3,0},{4,7},{5,6},{6,5},{7,4},{8,11},{9,10},{10,... | collective-permute-start | bytes 1179656 | tf_op jit(solution)/shard_map/ppermute | solution.py:410
  251.4 10.1 %copy-start.12 = (bf16[1024,192]{1,0:T(8,128)(2,1)}, bf16[1024,192]{1,0:T(8,128)(2,1)S(1)}, u32[]{:S(2)}) copy-start(bf16[1024,192]{1,0:T(8,128)(2,1)S(1)} %collective-permute-done.10.refs_6_) | copy-start | bytes 1179652
  261.5 0.8 copy-start.13
  262.3 102.5 %copy-start.4 = (bf16[768,3,256]{0,2,1:T(8,128)(2,1)S(1)}, bf16[768,3,256]{0,2,1:T(8,128)(2,1)}, u32[]{:S(2)}) copy-start(bf16[768,3,256]{0,2,1:T(8,128)(2,1)} %pad.8) | copy-start | bytes 3538948
  364.8 6.1 %copy-start.14 = (f32[32,768]{1,0:T(8,128)S(1)}, f32[32,768]{1,0:T(8,128)}, u32[]{:S(2)}) copy-start(f32[32,768]{1,0:T(8,128)} %get-tuple-element.52) | copy-start | bytes 294916
  368.8 11.8 %collective-permute-start.12 = (bf16[1024,768]{1,0:T(8,128)(2,1)}, bf16[1024,768]{1,0:T(8,128)(2,1)S(1)}, u32[]{:S(2)}, u32[]{:S(2)}) collective-permute-start(bf16[1024,768]{1,0:T(8,128)(2,1)} %convolution_convert_fusion.2), channel_id=1, source_target_pairs={{0,1},{1,0},{2,3},{3,2},{4,5},{5,4},{6,7},{7,6},{8,9},{9,8},{10,11... | collective-permute-start | bytes 4718600 | tf_op jit(solution)/shard_map/ppermute | solution.py:410
  375.2 63.4 %collective-permute-start.17 = (bf16[1024,768]{1,0:T(8,128)(2,1)}, bf16[1024,768]{1,0:T(8,128)(2,1)}, u32[]{:S(2)}, u32[]{:S(2)}) collective-permute-start(bf16[1024,768]{1,0:T(8,128)(2,1)} %convolution_convert_fusion), channel_id=1, source_target_pairs={{0,1},{1,0},{2,3},{3,2},{4,5},{5,4},{6,7},{7,6},{8,9},{9,8},{10,11... | collective-permute-start | bytes 4718600 | tf_op jit(solution)/shard_map/ppermute | solution.py:410
  380.2 10.7 %copy-start.7 = (bf16[432,768]{1,0:T(8,128)(2,1)S(1)}, bf16[432,768]{1,0:T(8,128)(2,1)}, u32[]{:S(2)}) copy-start(bf16[432,768]{1,0:T(8,128)(2,1)} %reduce-scatter.2.cloned.1.call-done) | copy-start | bytes 1990660
  380.2 10.7 %collective-permute-start.25 = (bf16[216,768]{1,0:T(8,128)(2,1)S(1)}, bf16[216,768]{1,0:T(8,128)(2,1)S(1)}, u32[]{:S(2)}, u32[]{:S(2)}) collective-permute-start(bf16[216,768]{1,0:T(8,128)(2,1)S(1)} %slice.166), channel_id=1, source_target_pairs={{0,2},{1,3},{2,0},{3,1},{4,6},{5,7},{6,4},{7,5},{8,10},{9,11},{10,... | collective-permute-start | bytes 995336 | tf_op jit(solution)/shard_map/ppermute | solution.py:410
  383.5 55.1 %collective-permute-start.18 = (bf16[1024,768]{1,0:T(8,128)(2,1)}, bf16[1024,768]{1,0:T(8,128)(2,1)}, u32[]{:S(2)}, u32[]{:S(2)}) collective-permute-start(bf16[1024,768]{1,0:T(8,128)(2,1)} %add_convert_fusion.1), channel_id=1, source_target_pairs={{0,2},{1,3},{2,0},{3,1},{4,6},{5,7},{6,4},{7,5},{8,10},{9,11},{10,... | collective-permute-start | bytes 4718600 | tf_op jit(solution)/shard_map/ppermute | solution.py:410
  391.7 10.3 %copy-start.6 = (bf16[768,3,192]{0,2,1:T(8,128)(2,1)S(1)}, bf16[768,3,192]{0,2,1:T(8,128)(2,1)}, u32[]{:S(2)}) copy-start(bf16[768,3,192]{0,2,1:T(8,128)(2,1)} %param.23) | copy-start | bytes 2654212
  391.7 10.3 %copy-start.19 = (f32[3]{0:T(128)S(1)}, f32[3]{0:T(128)}, u32[]{:S(2)}) copy-start(f32[3]{0:T(128)} %constant.103) | copy-start | bytes 40
  402.5 4.0 copy-start.15
  402.5 12.5 %collective-permute-start.13 = (bf16[384,576]{0,1:T(8,128)(2,1)S(1)}, bf16[384,576]{0,1:T(8,128)(2,1)}, u32[]{:S(2)}, u32[]{:S(2)}) collective-permute-start(bf16[384,576]{0,1:T(8,128)(2,1)S(1)} %bitcast.66), channel_id=1, source_target_pairs={{0,4},{4,0},{8,12},{12,8},{16,20},{20,16},{24,28},{28,24},{1,5},{5... | collective-permute-start | bytes 1327112 | tf_op jit(solution)/shard_map/ppermute | solution.py:410
  406.6 13.7 %collective-permute-start.26 = (f32[13,128]{1,0:T(8,128)S(1)}, f32[13,128]{1,0:T(8,128)S(1)}, u32[]{:S(2)}, u32[]{:S(2)}) collective-permute-start(f32[13,128]{1,0:T(8,128)S(1)} %pad_bitcast_fusion), channel_id=1, source_target_pairs={{0,1},{1,0},{2,3},{3,2},{4,5},{5,4},{6,7},{7,6},{8,9},{9,8},{10,11... | collective-permute-start | bytes 19976 | tf_op jit(solution)/shard_map/ppermute | solution.py:410
  416.4 9.6 %collective-permute-start.14 = (bf16[96,576]{0,1:T(8,128)(2,1)S(1)}, bf16[96,576]{0,1:T(8,128)(2,1)S(1)}, u32[]{:S(2)}, u32[]{:S(2)}) collective-permute-start(bf16[96,576]{0,1:T(8,128)(2,1)S(1)} %get-tuple-element.63), channel_id=1, source_target_pairs={{0,8},{4,12},{8,0},{12,4},{16,24},{20,28},{24,16},{28,20},{1,9},{5... | collective-permute-start | bytes 331784 | tf_op jit(solution)/shard_map/ppermute | solution.py:410
  416.4 21.9 %collective-permute-start.15 = (bf16[96,576]{0,1:T(8,128)(2,1)S(1)}, bf16[96,576]{0,1:T(8,128)(2,1)S(1)}, u32[]{:S(2)}, u32[]{:S(2)}) collective-permute-start(bf16[96,576]{0,1:T(8,128)(2,1)S(1)} %get-tuple-element.64), channel_id=1, source_target_pairs={{0,16},{4,20},{8,24},{12,28},{16,0},{20,4},{24,8},{28,12},{1,17},{... | collective-permute-start | bytes 331784 | tf_op jit(solution)/shard_map/ppermute | solution.py:410
  420.3 18.0 %collective-permute-start.16 = (bf16[96,576]{0,1:T(8,128)(2,1)S(1)}, bf16[96,576]{0,1:T(8,128)(2,1)S(1)}, u32[]{:S(2)}, u32[]{:S(2)}) collective-permute-start(bf16[96,576]{0,1:T(8,128)(2,1)S(1)} %get-tuple-element.65), channel_id=1, source_target_pairs={{0,24},{4,28},{8,16},{12,20},{16,8},{20,12},{24,0},{28,4},{1,25},{... | collective-permute-start | bytes 331784 | tf_op jit(solution)/shard_map/ppermute | solution.py:410
  426.0 33.4 %collective-permute-start.27 = (f32[13,128]{1,0:T(8,128)S(1)}, f32[13,128]{1,0:T(8,128)S(1)}, u32[]{:S(2)}, u32[]{:S(2)}) collective-permute-start(f32[13,128]{1,0:T(8,128)S(1)} %fusion.15), channel_id=1, source_target_pairs={{0,2},{1,3},{2,0},{3,1},{4,6},{5,7},{6,4},{7,5},{8,10},{9,11},{10,... | collective-permute-start | bytes 19976 | tf_op jit(solution)/shard_map/ppermute | solution.py:410
  445.7 27.2 %collective-permute-start.19 = (bf16[96,576]{0,1:T(8,128)(2,1)S(1)}, bf16[96,576]{0,1:T(8,128)(2,1)S(1)}, u32[]{:S(2)}, u32[]{:S(2)}) collective-permute-start(bf16[96,576]{0,1:T(8,128)(2,1)S(1)} %add_convert_fusion.4), channel_id=1, source_target_pairs={{0,24},{4,28},{8,16},{12,20},{16,8},{20,12},{24,0},{28,4},{1,25},{... | collective-permute-start | bytes 331784 | tf_op jit(solution)/shard_map/ppermute | solution.py:410
  450.0 22.9 %collective-permute-start.20 = (bf16[96,576]{0,1:T(8,128)(2,1)S(1)}, bf16[96,576]{0,1:T(8,128)(2,1)S(1)}, u32[]{:S(2)}, u32[]{:S(2)}) collective-permute-start(bf16[96,576]{0,1:T(8,128)(2,1)S(1)} %add_convert_fusion.4), channel_id=1, source_target_pairs={{0,16},{4,20},{8,24},{12,28},{16,0},{20,4},{24,8},{28,12},{1,17},{... | collective-permute-start | bytes 331784 | tf_op jit(solution)/shard_map/ppermute | solution.py:410
  458.8 14.1 %collective-permute-start.21 = (bf16[96,576]{0,1:T(8,128)(2,1)S(1)}, bf16[96,576]{0,1:T(8,128)(2,1)S(1)}, u32[]{:S(2)}, u32[]{:S(2)}) collective-permute-start(bf16[96,576]{0,1:T(8,128)(2,1)S(1)} %add_convert_fusion.4), channel_id=1, source_target_pairs={{0,8},{4,12},{8,0},{12,4},{16,24},{20,28},{24,16},{28,20},{1,9},{5... | collective-permute-start | bytes 331784 | tf_op jit(solution)/shard_map/ppermute | solution.py:410
  459.4 3.7 collective-permute-start.28
  463.1 3.9 collective-permute-start.29
  467.0 4.5 collective-permute-start.30
  473.2 8.4 %collective-permute-start.22 = (bf16[384,576]{0,1:T(8,128)(2,1)S(1)}, bf16[384,576]{0,1:T(8,128)(2,1)S(1)}, u32[]{:S(2)}, u32[]{:S(2)}) collective-permute-start(bf16[384,576]{0,1:T(8,128)(2,1)S(1)} %pad_maximum_fusion.1), channel_id=1, source_target_pairs={{0,4},{4,0},{8,12},{12,8},{16,20},{20,16},{24,28},{28,24},{1,5},{5... | collective-permute-start | bytes 1327112 | tf_op jit(solution)/shard_map/ppermute | solution.py:410
Sparse Core Ops, SparseCore 0:
  235.7 103.6 reduce-scatter.1
  391.8 68.4 all-gather.2
